TPU v7x, 512 devices: a whole 4x8x8 slice. The times are simulated.
512 devices in a mesh: seq: 128 (over z, y_lo, x), chan: 4 (over y_hi, core).
Axes of the slice: x: 4, y: 8 (y_hi: 2, y_lo: 4; y = y_hi * 4 + y_lo), z: 8, core: 2. Of those that a mesh axis runs over, the one named last changes fastest.
Arguments:
- inputs: bfloat16 [2, 960, 32768], P(None, 'chan', 'seq'), may hold values from -6 to 6
- first_blocks: bfloat16 [256, 128, 128], P('seq'), may hold values from -0.5 to 0.5
- second_blocks: bfloat16 [128, 256, 256], P('seq'), may hold values from -0.375 to 0.375
- kernel: float32 [3, 960], P(None, 'chan'), may hold values from -3 to 3
- cotangent: bfloat16 [2, 960, 32768], P(None, 'chan', 'seq'), may hold values from -6 to 6
Outputs:
- mixed: bfloat16 [2, 960, 32768], P(None, 'chan', 'seq')
- input_grad: bfloat16 [2, 960, 32768], P(None, 'chan', 'seq')
- kernel_grad: float32 [3, 960], P(None, 'chan')
- block_grad: float32 [256, 128, 128], P('seq', 'chan')
- factor_grad: float32 [128, 256, 256], P('seq', 'chan')
All inputs are finite; a program needn't handle non-finite values.
Results may differ from a plain program's by a relative error of at most 0.007.
Values may be sent and summed in bfloat16 or wider, within the bound.
A program may use at most 64 MiB of HBM per device.

v0:
```python
import jax
import jax.numpy as jnp
from jax import lax
from jax.sharding import PartitionSpec as P


def shifted(block, axis, distance):
    devices = range(lax.axis_size(axis))
    route = [(i - distance, i) for i in devices if i - distance in devices]
    return lax.ppermute(block, axis, route)


def tap_weight(kernel, tap_index):
    return kernel[tap_index][None, :, None]


def shards(inputs, first_blocks, second_blocks, kernel, cotangent):
    batches, channels, extent = inputs.shape
    block_count = first_blocks.shape[0]
    block_size = first_blocks.shape[1]
    tap_count = kernel.shape[0]
    rim_size = tap_count - 1
    blocked = inputs.reshape(batches, channels, block_count, block_size)
    mixed_in = jnp.einsum(
        "bcqp,qpr->bcrq", blocked, first_blocks, preferred_element_type=jnp.float32
    ).astype(jnp.bfloat16)
    pieces = lax.all_to_all(mixed_in, "seq", split_axis=2, concat_axis=3, tiled=True)
    result = jnp.einsum("bcpq,pqk->bcpk", pieces, second_blocks, preferred_element_type=jnp.float32)
    spread = pieces
    factor_out = result.astype(jnp.bfloat16)
    returned = lax.all_to_all(factor_out, "seq", split_axis=3, concat_axis=2, tiled=True)
    monarch = jnp.swapaxes(returned, 2, 3).reshape(batches, channels, extent).astype(jnp.float32)
    in_float = inputs.astype(jnp.float32)
    gated = (in_float * monarch).astype(jnp.bfloat16)
    gated_float = gated.astype(jnp.float32)
    prior = shifted(gated[:, :, extent - rim_size :], "seq", 1)
    extended = jnp.concatenate([prior, gated], axis=2).astype(jnp.float32)
    total = jnp.zeros((batches, channels, extent), jnp.float32)
    for tap_index in range(tap_count):
        start = rim_size - tap_index
        total = total + tap_weight(kernel, tap_index) * extended[:, :, start : start + extent]
    mixed = total.astype(jnp.bfloat16)
    head = shifted(cotangent[:, :, :rim_size], "seq", -1)
    after = jnp.concatenate([cotangent, head], axis=2).astype(jnp.float32)
    gate_grad = jnp.zeros((batches, channels, extent), jnp.float32)
    kernel_rows = []
    for tap_index in range(tap_count):
        window = after[:, :, tap_index : tap_index + extent]
        gate_grad = gate_grad + tap_weight(kernel, tap_index) * window
        kernel_rows.append(jnp.sum(gated_float * window, axis=(0, 2)))
    kernel_grad = lax.psum(jnp.stack(kernel_rows), "seq")
    direct = gate_grad * monarch
    monarch_grad = (gate_grad * in_float).astype(jnp.bfloat16)
    adjoint_in = jnp.swapaxes(
        monarch_grad.reshape(batches, channels, block_count, block_size), 2, 3
    )
    pieces = lax.all_to_all(adjoint_in, "seq", split_axis=2, concat_axis=3, tiled=True)
    result = jnp.einsum("bcpk,pqk->bcpq", pieces, second_blocks, preferred_element_type=jnp.float32)
    mixed_grad = result.astype(jnp.bfloat16)
    grad_back = lax.all_to_all(mixed_grad, "seq", split_axis=3, concat_axis=2, tiled=True)
    through = jnp.einsum(
        "bcrq,qpr->bcqp", grad_back, first_blocks, preferred_element_type=jnp.float32
    )
    input_grad = (direct + through.reshape(batches, channels, extent)).astype(jnp.bfloat16)
    block_term = jnp.einsum(
        "bcqp,bcrq->qpr", blocked, grad_back, preferred_element_type=jnp.float32
    )
    factor_term = jnp.einsum("bcpq,bcpk->pqk", spread, pieces, preferred_element_type=jnp.float32)
    factor_grad, block_grad = (
        lax.psum_scatter(factor_term, "chan", scatter_dimension=1, tiled=True),
        lax.psum_scatter(block_term, "chan", scatter_dimension=1, tiled=True),
    )
    return (mixed, input_grad, kernel_grad, block_grad, factor_grad)


def solution(mesh):
    placed = (
        P(None, "chan", "seq"),
        P("seq", None, None),
        P("seq", None, None),
        P(None, "chan"),
        P(None, "chan", "seq"),
    )
    return jax.shard_map(
        shards,
        mesh=mesh,
        in_specs=placed,
        out_specs=(
            P(None, "chan", "seq"),
            P(None, "chan", "seq"),
            P(None, "chan"),
            P("seq", "chan", None),
            P("seq", "chan", None),
        ),
        check_vma=False,
    )
```

profile of v0, /device:TPU:1, one launch (start us, length us, event | category | flops | bytes accessed | tf_op | source)
XLA Modules:
  0.0 576.1 jit_solution(4153852165750025939)
XLA Ops:
  7.2 0.0 copy-start
  7.2 1.0 copy_bitcast_fusion
  8.2 0.2 fusion.16
  8.5 0.2 copy.47
  8.7 30.4 %all_to_all.19 = bf16[2,240,128,2]{1,0,3,2:T(2,128)(2,1)S(1)} all-to-all(bf16[2,240,128,2]{1,0,3,2:T(2,128)(2,1)S(1)} %copy.47), channel_id=1, replica_groups=mesh['seq'=128,'chan'=4] {'seq'}, dimensions={2} | all-to-all | bytes 491520 | tf_op jit(solution)/shard_map/all_to_all | solution.py:27
  39.1 0.2 copy.48
  39.2 0.2 fusion
  39.5 0.9 copy.49
  40.3 8.3 %all-to-all-start.1 = ((bf16[2,240,1,256]{1,0,2,3:T(2,128)(2,1)}), bf16[2,240,1,256]{1,0,2,3:T(2,128)(2,1)S(1)}, u32[]{:S(2)}, u32[]{:S(2)}) async-start(bf16[2,240,1,256]{1,0,2,3:T(2,128)(2,1)} %copy.49), calls=%async_computation.1 | async-start | bytes 524288 | tf_op jit(solution)/shard_map/all_to_all | solution.py:31
  48.6 0.0 copy-start.4
  48.6 1.3 collective-permute-start.1
  50.0 5.5 collective-permute-done.1
  55.4 0.1 maximum_convert_fusion.1
  55.5 4.8 all-to-all-done.1
  60.3 0.2 convert_bitcast_fusion
  60.5 0.8 copy.50
  61.3 0.0 copy-start.1
  61.3 0.4 reshape.66
  61.7 0.5 copy-done.1
  62.2 0.7 fusion.3
  62.9 0.1 reshape.63
  63.0 0.7 copy.51
  63.7 23.5 %all_to_all.40 = bf16[2,240,128,2]{1,0,3,2:T(2,128)(2,1)S(1)} all-to-all(bf16[2,240,128,2]{1,0,3,2:T(2,128)(2,1)S(1)} %bitcast.80), channel_id=1, replica_groups=mesh['seq'=128,'chan'=4] {'seq'}, dimensions={2} | all-to-all | bytes 491520 | tf_op jit(solution)/shard_map/all_to_all | solution.py:57
  87.2 0.2 copy.52
  87.3 0.3 fusion.1
  87.6 0.9 copy.53
  88.5 6.2 %all-to-all-start.3 = ((bf16[2,240,1,256]{1,0,2,3:T(2,128)(2,1)}), bf16[2,240,1,256]{1,0,2,3:T(2,128)(2,1)S(1)}, u32[]{:S(2)}, u32[]{:S(2)}) async-start(bf16[2,240,1,256]{1,0,2,3:T(2,128)(2,1)} %copy.53), calls=%async_computation.3 | async-start | bytes 524288 | tf_op jit(solution)/shard_map/all_to_all | solution.py:60
  94.7 0.0 all-reduce.3.cloned.1.call-start
  94.7 1.3 dynamic-slice
  96.6 0.1 slice.47
  96.7 2.5 collective-permute-start
  99.2 312.8 %psum.7 = f32[3,240]{1,0:T(4,128)} all-reduce(f32[3,240]{1,0:T(4,128)S(1)} %pad_maximum_fusion), channel_id=1, replica_groups=mesh['seq'=128,'chan'=4] {'seq'}, use_global_device_ids=true, to_apply=%region_3.0 | all-reduce | flops 720 | bytes 5760 | tf_op jit(solution)/shard_map/psum | solution.py:51
  412.0 0.0 collective-permute-done
  412.0 0.2 maximum_convert_fusion
  412.2 0.2 copy.54
  412.5 0.3 convolution_bitcast_fusion.2
  412.8 0.7 copy.58
  413.5 0.0 all-reduce.3.cloned.1.call-update
  413.5 0.0 reduce-scatter.2.cloned.1.call-start
  413.6 1.0 convolution_bitcast_fusion.1
  414.5 0.0 reduce-scatter.2.cloned.1.call-update
  414.6 1.1 fusion.9
  415.7 0.2 convolution_bitcast_fusion
  415.9 0.8 fusion.7
  416.7 111.1 %all-reduce.3.cloned.1.call-done = f32[2,128,128]{2,0,1:T(2,128)} async-done(((f32[2,128,128]{2,0,1:T(2,128)}), f32[2,128,128]{2,0,1:T(2,128)}) %all-reduce.3.cloned.1.call-update) | async-done | bytes 131088
  527.8 0.8 constant_dynamic-slice_fusion
  528.6 0.6 copy.61
  529.2 40.1 %reduce-scatter.2.cloned.1.call-done = f32[1,64,256]{2,1,0:T(8,128)} async-done(((f32[1,256,256]{2,1,0:T(8,128)}), f32[1,64,256]{2,1,0:T(8,128)}) %reduce-scatter.2.cloned.1.call-update) | async-done | bytes 65552 | tf_op jit(solution)/shard_map/reduce_scatter | solution.py:70
  (11 shorter events, 0.1 us)
Async XLA Ops:
  7.2 32.1 %copy-start = (bf16[1,256,256]{2,1,0:T(8,128)(2,1)S(1)}, bf16[1,256,256]{2,1,0:T(8,128)(2,1)}, u32[]{:S(2)}) copy-start(bf16[1,256,256]{2,1,0:T(8,128)(2,1)} %param.7) | copy-start | bytes 393220
  7.2 1.1 copy-start.3
  40.3 8.3 %copy-start.2 = (bf16[2,240,256]{2,1,0:T(8,128)(2,1)S(1)}, bf16[2,240,256]{2,1,0:T(8,128)(2,1)}, u32[]{:S(2)}) copy-start(bf16[2,240,256]{2,1,0:T(8,128)(2,1)} %param.9) | copy-start | bytes 737284
  40.3 20.0 %all-to-all-start.1 = ((bf16[2,240,1,256]{1,0,2,3:T(2,128)(2,1)}), bf16[2,240,1,256]{1,0,2,3:T(2,128)(2,1)S(1)}, u32[]{:S(2)}, u32[]{:S(2)}) async-start(bf16[2,240,1,256]{1,0,2,3:T(2,128)(2,1)} %copy.49), calls=%async_computation.1 | async-start | bytes 524288 | tf_op jit(solution)/shard_map/all_to_all | solution.py:31
  48.6 1.3 copy-start.4
  48.6 6.8 %collective-permute-start.1 = (bf16[2,240,2]{2,1,0:T(8,128)(2,1)S(1)}, bf16[2,240,2]{2,1,0:T(8,128)(2,1)S(1)}, u32[]{:S(2)}, u32[]{:S(2)}) collective-permute-start(bf16[2,240,2]{2,1,0:T(8,128)(2,1)S(1)} %slice.43), channel_id=1, source_target_pairs={{4,0},{8,4},{12,8},{16,12},{20,16},{24,20},{28,24},{32,28},{36,32}... | collective-permute-start | bytes 5768 | tf_op jit(solution)/shard_map/ppermute | solution.py:10
  61.3 0.9 copy-start.1
  88.5 323.8 %all-to-all-start.3 = ((bf16[2,240,1,256]{1,0,2,3:T(2,128)(2,1)}), bf16[2,240,1,256]{1,0,2,3:T(2,128)(2,1)S(1)}, u32[]{:S(2)}, u32[]{:S(2)}) async-start(bf16[2,240,1,256]{1,0,2,3:T(2,128)(2,1)} %copy.53), calls=%async_computation.3 | async-start | bytes 524288 | tf_op jit(solution)/shard_map/all_to_all | solution.py:60
  94.7 433.1 %all-reduce.3.cloned.1.call-start = ((), (), s32[]{:S(2)}) async-start(), calls=%async_computation.6 | async-start | bytes 262144
  96.7 315.3 %collective-permute-start = (bf16[2,240,2]{2,1,0:T(8,128)(2,1)S(1)}, bf16[2,240,2]{2,1,0:T(8,128)(2,1)S(1)}, u32[]{:S(2)}, u32[]{:S(2)}) collective-permute-start(bf16[2,240,2]{2,1,0:T(8,128)(2,1)S(1)} %slice.47), channel_id=1, source_target_pairs={{0,4},{4,8},{8,12},{12,16},{16,20},{20,24},{24,28},{28,32},{32,36}... | collective-permute-start | bytes 5768 | tf_op jit(solution)/shard_map/ppermute | solution.py:10
  413.5 155.7 %reduce-scatter.2.cloned.1.call-start = ((), (), s32[]{:S(2)}) async-start(), calls=%async_computation.5 | async-start | bytes 327680 | tf_op jit(solution)/shard_map/reduce_scatter | solution.py:70
Sparse Core Ops, SparseCore 0:
  413.7 114.0 all-reduce.2
  531.6 37.5 reduce-scatter.1
where the time goes:
time: 577 us; the launch traced here: 576 us
  blocking collectives  367 us (64%)
  waiting for transfers between devices  162 us (28%)
  starting transfers between devices  18.3 us (3%)
  between operations  14.9 us (3%)
  local copies, waits for them, and re-layouts  9.49 us (2%)
    psum x1, blocking collectives, shards(): kernel_grad = lax.psum(jnp.stack(kernel_rows), 'seq')  313 us
    unnamed x3, waiting for transfers between devices  111 us
    reduce_scatter x1, waiting for transfers between devices, shards(): lax.psum_scatter(factor_term, 'chan', scatter_dimension=1, tiled=True)  40.1 us
    all_to_all x1, blocking collectives, shards(): lax.all_to_all(mixed_in, 'seq', split_axis=2, concat_axis=3, tiled=True)  30.4 us
    all_to_all x1, blocking collectives, shards(): lax.all_to_all(adjoint_in, 'seq', split_axis=2, concat_axis=3, tiled=True)  23.5 us
  transfers between devices with their start and end apart: 6, of which 4 were waited for; matrix products, arithmetic and copies ran while one was open for 1% of the time, Pallas kernels for 0%

commit v1 on v0

v1 whole, which is shorter than its diff:
```python
import jax
import jax.numpy as jnp
from jax import lax
from jax.experimental import pallas as pl
from jax.experimental.pallas import tpu as pltpu
from jax.sharding import PartitionSpec as P

NX, NL = 8, 16
SEQ, CHAN = NX * NL, 4
BATCH, CH, EXT, BLK = 2, 240, 256, 128
ROWS = BATCH * CH
LANES = 512
MESH = pl.DeviceIdType.MESH
BF, F32 = jnp.bfloat16, jnp.float32


def dot(a, b, ca, cb):
    return lax.dot_general(a, b, (((ca,), (cb,)), ((), ())), preferred_element_type=F32)


def nn(a, b):
    return dot(a, b, 1, 0)


def nt(a, b):
    return dot(a, b, 1, 1)


def tn(a, b):
    return dot(a, b, 0, 0)


def hot(shape, where):
    row = lax.broadcasted_iota(jnp.int32, shape, 0)
    col = lax.broadcasted_iota(jnp.int32, shape, 1)
    return jnp.where(where(row, col), 1.0, 0.0).astype(BF)


def place0(r, c):
    return ((r >> 4) & 1) * 128 + (r & 15) * 8 + (r >> 5) == c


def turn0(r, c):
    return ((r >> 1) & 7) * 32 + (r & 1) * 16 + (r >> 4) == c


def place1(r, c):
    return ((r >> 3) & 1) * 128 + (r >> 4) * 8 + (r & 7) == c


def turn1(r, c):
    return ((r >> 1) & 15) * 16 + (r & 1) * 8 + (r >> 5) == c


def order1(r, c):
    return ((r >> 1) & 7) * 32 + (r >> 4) * 2 + (r & 1) == c


def flip(where):
    return lambda r, c: where(c, r)


def body(
    x_ref, f_ref, s_ref, k_ref, c_ref,
    mixed_ref, igrad_ref, kgrad_ref, bgrad_ref, fgrad_ref,
    xs, cs, xt, gate, kpad, kcol, prod_w, st, s11, mgr,
    a0s, a0r, b0s, b0r, b1s, b1r, a1s, a1r,
    b2s, b2r, a2s, a2r, a3s, a3r, b3s, b3r,
    h0s, h0r, h1s, h1r,
    kxs, kxr, kls, klr, fgs, fgr, bgs, bgr,
    ssem, rsem,
):
    seq = lax.axis_index("seq")
    chan = lax.axis_index("chan")
    mx = lax.rem(seq, NX)
    ml = lax.div(seq, NX)
    ahead = lax.rem(seq + 1, SEQ)
    behind = lax.rem(seq + SEQ - 1, SEQ)

    def x_peer(d):
        other = lax.rem(mx + d, NX)
        return other, (ml * NX + other, chan)

    def l_peer(d):
        other = lax.rem(ml + d, NL)
        return other, (other * NX + mx, chan)

    def c_peer(d):
        other = lax.rem(chan + d, CHAN)
        return other, (seq, other)

    barrier = pltpu.get_barrier_semaphore()

    def greet(peer, count):
        def step(d, carry):
            pl.semaphore_signal(barrier, inc=1, device_id=peer(d)[1], device_id_type=MESH)
            return carry

        lax.fori_loop(1, count, step, 0)

    greet(x_peer, NX)
    greet(l_peer, NL)
    greet(c_peer, CHAN)
    pl.semaphore_signal(barrier, inc=1, device_id=(ahead, chan), device_id_type=MESH)
    pl.semaphore_signal(barrier, inc=1, device_id=(behind, chan), device_id_type=MESH)

    def scatter(send, recv, mine, peer, count, sem):
        def step(d, carry):
            other, device = peer(d)
            pltpu.make_async_remote_copy(
                src_ref=send.at[other], dst_ref=recv.at[mine],
                send_sem=ssem.at[sem], recv_sem=rsem.at[sem],
                device_id=device, device_id_type=MESH,
            ).start()
            return carry

        lax.fori_loop(1, count, step, 0)
        recv[mine] = send[mine]

    def arrive(recv, count, sem):
        part = recv.at[pl.ds(0, count - 1)]
        pltpu.make_async_copy(part, part, rsem.at[sem]).wait()

    def sent(send, count, sem):
        part = send.at[pl.ds(0, count - 1)]
        pltpu.make_async_copy(part, part, ssem.at[sem]).wait()

    def spread(send, recv, mine, peer, count, sem):
        def step(d, carry):
            other, device = peer(d)
            pltpu.make_async_remote_copy(
                src_ref=send, dst_ref=recv.at[mine],
                send_sem=ssem.at[sem], recv_sem=rsem.at[sem],
                device_id=device, device_id_type=MESH,
            ).start()
            return carry

        lax.fori_loop(1, count, step, 0)
        recv[mine] = send[...]

    def hand(send, recv, device, sem):
        copy = pltpu.make_async_remote_copy(
            src_ref=send, dst_ref=recv, send_sem=ssem.at[sem], recv_sem=rsem.at[sem],
            device_id=(device, chan), device_id_type=MESH,
        )
        copy.start()
        return copy

    def flat(ref):
        return ref[...].reshape(256, LANES)

    zero_rows = jnp.zeros((LANES - ROWS, EXT), BF)
    xs[0:ROWS, :] = x_ref[...].reshape(ROWS, EXT)
    xs[ROWS:LANES, :] = zero_rows
    cs[0:ROWS, :] = c_ref[...].reshape(ROWS, EXT)
    cs[ROWS:LANES, :] = zero_rows

    h0s[...] = nt(hot((16, EXT), lambda r, c: (r == c) & (r < 2)), cs[...]).astype(BF)
    m0 = nn(xs[:, 0:BLK], f_ref[0]).astype(BF)
    m1 = nn(xs[:, BLK:EXT], f_ref[1]).astype(BF)
    p0 = hot((256, 256), place0)
    a0s[...] = (nt(p0[:, 0:BLK], m0) + nt(p0[:, BLK:EXT], m1)).astype(BF).reshape(NX, 32, LANES)

    pl.semaphore_wait(barrier, NX - 1 + NL - 1 + CHAN - 1 + 2)

    halo0 = hand(h0s, h0r, behind, 16)
    scatter(a0s, a0r, mx, x_peer, NX, 0)

    kpad[...] = jnp.zeros_like(kpad)
    kpad[0:3, 0:CH] = k_ref[...]
    taps = jnp.concatenate([kpad[:, 0:128].T, kpad[:, 128:256].T], axis=0)
    kcol[0:CH, :] = taps[0:CH]
    kcol[CH:ROWS, :] = taps[0:CH]
    kcol[ROWS:LANES, :] = jnp.zeros((LANES - ROWS, 128), F32)

    cot = cs[...]
    near1 = nn(cot, hot((EXT, EXT), lambda r, c: r == c + 1))
    near2 = nn(cot, hot((EXT, EXT), lambda r, c: r == c + 2))
    halo0.wait_recv()
    keep = (seq < SEQ - 1).astype(F32)
    tail = (h0r[...].astype(F32) * keep).astype(BF)
    near1 = near1 + tn(tail, hot((16, EXT), lambda r, c: (r == 0) & (c == EXT - 1)))
    near2 = near2 + tn(tail, hot((16, EXT), lambda r, c: (r < 2) & (c == EXT - 2 + r)))
    prod_w[0] = near1.astype(BF)
    prod_w[1] = near2.astype(BF)
    gate[...] = kcol[:, 0:1] * cot.astype(F32) + kcol[:, 1:2] * near1 + kcol[:, 2:3] * near2
    mgrad = (gate[...] * xs[...].astype(F32)).astype(BF)
    b1s[...] = nt(hot((256, 256), place1), mgrad).astype(BF).reshape(NL, 16, LANES)
    scatter(b1s, b1r, ml, l_peer, NL, 1)

    eye = hot((256, 256), lambda r, c: r == c)
    second = s_ref[0]
    st[...] = nt(eye, second).astype(BF)
    back = hot((256, 256), flip(order1))
    s11[...] = nt(nn(back, second).astype(BF), back).astype(BF)
    xt[...] = nt(eye, xs[...]).astype(BF)

    arrive(a0r, NX, 0)
    b0s[...] = nn(hot((256, 256), turn0), flat(a0r)).astype(BF).reshape(NL, 16, LANES)
    scatter(b0s, b0r, ml, l_peer, NL, 2)

    arrive(b1r, NL, 1)
    a1s[...] = nn(hot((256, 256), turn1), flat(b1r)).astype(BF).reshape(NX, 32, LANES)
    scatter(a1s, a1r, mx, x_peer, NX, 3)

    arrive(b0r, NL, 2)
    b2s[...] = nn(st[...], flat(b0r)).astype(BF).reshape(NL, 16, LANES)
    scatter(b2s, b2r, ml, l_peer, NL, 4)

    arrive(a1r, NX, 3)
    a3s[...] = nn(s11[...], flat(a1r)).astype(BF).reshape(NX, 32, LANES)
    scatter(a3s, a3r, mx, x_peer, NX, 5)

    mg_nat = nn(hot((256, 256), order1), flat(a1r)).astype(BF)
    fgs[...] = nt(flat(b0r), mg_nat).reshape(CHAN, 64, 256)
    scatter(fgs, fgr, chan, c_peer, CHAN, 6)

    arrive(b2r, NL, 4)
    a2s[...] = nn(hot((256, 256), flip(turn0)), flat(b2r)).astype(BF).reshape(NX, 32, LANES)
    scatter(a2s, a2r, mx, x_peer, NX, 7)

    arrive(a3r, NX, 5)
    b3s[...] = nn(hot((256, 256), flip(turn1)), flat(a3r)).astype(BF).reshape(NL, 16, LANES)
    scatter(b3s, b3r, ml, l_peer, NL, 8)

    arrive(a2r, NX, 7)
    monarch = tn(flat(a2r), hot((256, 256), place0))
    gated = (xs[...].astype(F32) * monarch).astype(BF)
    h1s[...] = nt(hot((16, EXT), lambda r, c: (r < 2) & (c == EXT - 2 + r)), gated).astype(BF)
    halo1 = hand(h1s, h1r, ahead, 17)
    gate[...] = gate[...] * monarch

    gated32 = gated.astype(F32)
    kg = jnp.zeros((8, CH), F32)
    for j in range(3):
        pick = hot((8, EXT), lambda r, c: (r == j) & (c >= 0))
        window = cs[...] if j == 0 else prod_w[j - 1]
        prod = gated32 * window.astype(F32)
        high = prod.astype(BF)
        low = (prod - high.astype(F32)).astype(BF)
        for b in range(BATCH):
            rows = slice(b * CH, (b + 1) * CH)
            kg = kg + nt(pick, high[rows]) + nt(pick, low[rows])
    kxs[...] = jnp.zeros_like(kxs)
    kxs[:, 0:CH] = kg
    spread(kxs, kxr, mx, x_peer, NX, 9)

    far1 = nn(gated, hot((EXT, EXT), lambda r, c: r + 1 == c))
    far2 = nn(gated, hot((EXT, EXT), lambda r, c: r + 2 == c))
    total = kcol[:, 0:1] * gated32 + kcol[:, 1:2] * far1 + kcol[:, 2:3] * far2

    arrive(b3r, NL, 8)
    mgr[...] = tn(flat(b3r), hot((256, 256), place1)).astype(BF)
    for q in range(2):
        lanes = slice(q * BLK, (q + 1) * BLK)
        part = nn(xt[lanes, :], mgr[:, lanes]).reshape(CHAN, 32, BLK)
        for o in range(CHAN):
            bgs[o, q] = part[o]
    scatter(bgs, bgr, chan, c_peer, CHAN, 10)

    arrive(kxr, NX, 9)
    kls[...] = sum((kxr[i] for i in range(1, NX)), kxr[0])
    spread(kls, klr, ml, l_peer, NL, 11)

    for q in range(2):
        lanes = slice(q * BLK, (q + 1) * BLK)
        through = nt(mgr[:, lanes], f_ref[q])
        out = (gate[:, lanes] + through)[0:ROWS].astype(BF)
        igrad_ref[:, :, lanes] = out.reshape(BATCH, CH, BLK)

    halo1.wait_recv()
    keep = (seq > 0).astype(F32)
    prior = (h1r[...].astype(F32) * keep).astype(BF)
    edge1 = tn(prior, hot((16, EXT), lambda r, c: (r == 1) & (c == 0)))
    edge2 = tn(prior, hot((16, EXT), lambda r, c: (r < 2) & (r == c)))
    total = total + (kcol[:, 1:2] * edge1 + kcol[:, 2:3] * edge2)
    mixed_ref[...] = total[0:ROWS].astype(BF).reshape(BATCH, CH, EXT)

    arrive(fgr, CHAN, 6)
    fgrad_ref[0] = (fgr[0] + fgr[1]) + (fgr[2] + fgr[3])
    arrive(bgr, CHAN, 10)
    bgrad_ref[...] = (bgr[0] + bgr[1]) + (bgr[2] + bgr[3])
    arrive(klr, NL, 11)
    whole = sum((klr[i] for i in range(1, NL)), klr[0])
    kgrad_ref[...] = whole[0:3, 0:CH]

    halo0.wait_send()
    halo1.wait_send()
    sent(a0s, NX, 0)
    sent(b1s, NL, 1)
    sent(b0s, NL, 2)
    sent(a1s, NX, 3)
    sent(b2s, NL, 4)
    sent(a3s, NX, 5)
    sent(fgs, CHAN, 6)
    sent(a2s, NX, 7)
    sent(b3s, NL, 8)
    sent(kxr, NX, 9)
    sent(bgs, CHAN, 10)
    sent(klr, NL, 11)


def shards(inputs, first_blocks, second_blocks, kernel, cotangent):
    vmem = pl.BlockSpec(memory_space=pltpu.VMEM)
    xbuf = pltpu.VMEM((NX, 32, LANES), BF)
    lbuf = pltpu.VMEM((NL, 16, LANES), BF)
    halo = pltpu.VMEM((16, LANES), BF)
    return pl.pallas_call(
        body,
        out_shape=(
            jax.ShapeDtypeStruct((BATCH, CH, EXT), BF),
            jax.ShapeDtypeStruct((BATCH, CH, EXT), BF),
            jax.ShapeDtypeStruct((3, CH), F32),
            jax.ShapeDtypeStruct((2, BLK // CHAN, BLK), F32),
            jax.ShapeDtypeStruct((1, 256 // CHAN, 256), F32),
        ),
        in_specs=[vmem] * 5,
        out_specs=(vmem,) * 5,
        scratch_shapes=[
            pltpu.VMEM((LANES, EXT), BF),
            pltpu.VMEM((LANES, EXT), BF),
            pltpu.VMEM((EXT, LANES), BF),
            pltpu.VMEM((LANES, EXT), F32),
            pltpu.VMEM((128, 256), F32),
            pltpu.VMEM((LANES, 128), F32),
            pltpu.VMEM((2, LANES, EXT), BF),
            pltpu.VMEM((256, 256), BF),
            pltpu.VMEM((256, 256), BF),
            pltpu.VMEM((LANES, EXT), BF),
            xbuf, xbuf, lbuf, lbuf, lbuf, lbuf, xbuf, xbuf,
            lbuf, lbuf, xbuf, xbuf, xbuf, xbuf, lbuf, lbuf,
            halo, halo, halo, halo,
            pltpu.VMEM((8, 256), F32), pltpu.VMEM((NX, 8, 256), F32),
            pltpu.VMEM((8, 256), F32), pltpu.VMEM((NL, 8, 256), F32),
            pltpu.VMEM((CHAN, 64, 256), F32), pltpu.VMEM((CHAN, 64, 256), F32),
            pltpu.VMEM((CHAN, 2, 32, BLK), F32), pltpu.VMEM((CHAN, 2, 32, BLK), F32),
            pltpu.SemaphoreType.DMA((18,)),
            pltpu.SemaphoreType.DMA((18,)),
        ],
        compiler_params=pltpu.CompilerParams(
            collective_id=0, has_side_effects=True, vmem_limit_bytes=40 * 1024 * 1024
        ),
    )(inputs, first_blocks, second_blocks, kernel, cotangent)


def solution(mesh):
    placed = (
        P(None, "chan", "seq"),
        P("seq", None, None),
        P("seq", None, None),
        P(None, "chan"),
        P(None, "chan", "seq"),
    )
    return jax.shard_map(
        shards,
        mesh=mesh,
        in_specs=placed,
        out_specs=(
            P(None, "chan", "seq"),
            P(None, "chan", "seq"),
            P(None, "chan"),
            P("seq", "chan", None),
            P("seq", "chan", None),
        ),
        check_vma=False,
    )
```

time: 577 us -> 72.5 us (0.13)
  blocking collectives: 367 us -> 0 us
  waiting for transfers between devices: 162 us -> 0 us
  Pallas kernels: 0 us -> 63 us
  starting transfers between devices: 18.3 us -> 0 us
  between operations: 14.9 us -> 0.66 us
    psum x1 -> x0, blocking collectives: 313 us -> none  [shards(): kernel_grad = lax.psum(jnp.stack(kernel_rows), 'seq')]
    unnamed x3 -> x0, waiting for transfers between devices: 111 us -> none
    pallas_call x0 -> x1, Pallas kernels: none -> 63 us  [shards(): pl.pallas_call(body, out_shape=(jax.ShapeDtypeStruct((BATCH, CH, EXT), BF...]
    all_to_all x2 -> x0, blocking collectives: 53.9 us -> none  [the longest x1 30.4 us: shards(): lax.all_to_all(mixed_in, 'seq', split_axis=2, concat_axis=3, tiled=True)]
    reduce_scatter x1 -> x0, waiting for transfers between devices: 40.1 us -> none  [shards(): lax.psum_scatter(factor_term, 'chan', scatter_dimension=1, tiled=True)]
    all_to_all x2 -> x0, starting transfers between devices: 14.5 us -> none  [the longest x1 8.27 us: shards(): lax.all_to_all(factor_out, 'seq', split_axis=3, concat_axis=2, tiled=True)]
  transfers between devices with their start and end apart: 6 -> 0, of which waited for: 4 -> 0; matrix products, arithmetic and copies ran while one was open for 1% -> 0% of each run, Pallas kernels for 0% -> 0%
where the time goes in v1:
time: 72.5 us; the launch traced here: 71.2 us
  Pallas kernels  63 us (87%)
  local copies, waits for them, and re-layouts  7.53 us (10%)
    pallas_call x1, Pallas kernels, shards(): pl.pallas_call(body, out_shape=(jax.ShapeDtypeStruct((BATCH, CH, EXT), BF...  63 us
    unnamed x15, local copies, waits for them, and re-layouts  7.53 us

profile of v1, /device:TPU:1, one launch (start us, length us, event | category | flops | bytes accessed | tf_op | source)
XLA Modules:
  0.0 71.2 jit_solution(1717841625837466243)
XLA Ops:
  0.6 0.0 copy-start
  0.6 0.9 %copy-done = bf16[2,240,256]{2,1,0:T(8,128)(2,1)S(1)} copy-done((bf16[2,240,256]{2,1,0:T(8,128)(2,1)S(1)}, bf16[2,240,256]{2,1,0:T(8,128)(2,1)}, u32[]{:S(2)}) %copy-start) | copy-done | bytes 245784
  1.6 0.0 copy-start.1
  1.6 0.9 %copy-done.1 = bf16[2,240,256]{2,1,0:T(8,128)(2,1)S(1)} copy-done((bf16[2,240,256]{2,1,0:T(8,128)(2,1)S(1)}, bf16[2,240,256]{2,1,0:T(8,128)(2,1)}, u32[]{:S(2)}) %copy-start.1) | copy-done | bytes 245784
  2.5 0.0 copy-start.2
  2.5 0.9 %copy-done.2 = bf16[1,256,256]{2,1,0:T(8,128)(2,1)S(1)} copy-done((bf16[1,256,256]{2,1,0:T(8,128)(2,1)S(1)}, bf16[1,256,256]{2,1,0:T(8,128)(2,1)}, u32[]{:S(2)}) %copy-start.2) | copy-done | bytes 131096
  3.4 0.0 copy-start.3
  3.4 0.8 %copy-done.3 = bf16[2,128,128]{2,1,0:T(8,128)(2,1)S(1)} copy-done((bf16[2,128,128]{2,1,0:T(8,128)(2,1)S(1)}, bf16[2,128,128]{2,1,0:T(8,128)(2,1)}, u32[]{:S(2)}) %copy-start.3) | copy-done | bytes 65560
  4.3 0.0 copy-start.4
  4.3 0.7 copy-done.4
  5.0 63.0 %shard_map.92 = (bf16[2,240,256]{2,1,0:T(8,128)(2,1)S(1)}, bf16[2,240,256]{2,1,0:T(8,128)(2,1)S(1)}, f32[3,240]{1,0:T(4,128)S(1)}, f32[2,32,128]{2,1,0:T(8,128)S(1)}, f32[1,64,256]{2,1,0:T(8,128)S(1)}) custom-call(bf16[2,240,256]{2,1,0:T(8,128)(2,1)S(1)} %copy-done, bf16[2,128,128]{2,1,0:T(8,128)(2,1)S(1)} %copy-done.3, bf16[1,256,256]{2,1,0:T(8,128)(2,1)S(1)} %copy-done.2, ...), custom_call_target="tpu_custom_call" | custom-call | tf_op jit(solution)/shard_map/pallas_call | solution.py:308
  68.0 0.7 copy.15
  68.7 0.7 copy.16
  69.4 0.6 copy.17
  69.9 0.6 copy.18
  70.6 0.6 copy.19
Async XLA Ops:
  0.6 0.9 %copy-start = (bf16[2,240,256]{2,1,0:T(8,128)(2,1)S(1)}, bf16[2,240,256]{2,1,0:T(8,128)(2,1)}, u32[]{:S(2)}) copy-start(bf16[2,240,256]{2,1,0:T(8,128)(2,1)} %x_ref.1) | copy-start | bytes 737284
  1.6 0.9 %copy-start.1 = (bf16[2,240,256]{2,1,0:T(8,128)(2,1)S(1)}, bf16[2,240,256]{2,1,0:T(8,128)(2,1)}, u32[]{:S(2)}) copy-start(bf16[2,240,256]{2,1,0:T(8,128)(2,1)} %c_ref.1) | copy-start | bytes 737284
  2.5 0.9 %copy-start.2 = (bf16[1,256,256]{2,1,0:T(8,128)(2,1)S(1)}, bf16[1,256,256]{2,1,0:T(8,128)(2,1)}, u32[]{:S(2)}) copy-start(bf16[1,256,256]{2,1,0:T(8,128)(2,1)} %s_ref.1) | copy-start | bytes 393220
  3.4 0.8 %copy-start.3 = (bf16[2,128,128]{2,1,0:T(8,128)(2,1)S(1)}, bf16[2,128,128]{2,1,0:T(8,128)(2,1)}, u32[]{:S(2)}) copy-start(bf16[2,128,128]{2,1,0:T(8,128)(2,1)} %f_ref.1) | copy-start | bytes 196612
  4.3 0.7 copy-start.4

commit v2 on v0

v2 whole, which is shorter than its diff:
```python
import jax
import jax.numpy as jnp
from jax import lax
from jax.experimental import pallas as pl
from jax.experimental.pallas import tpu as pltpu
from jax.sharding import PartitionSpec as P

NX, NL = 8, 16
SEQ, CHAN = NX * NL, 4
BATCH, CH, EXT, BLK = 2, 240, 256, 128
ROWS = 256
MESH = pl.DeviceIdType.MESH
BF, F32 = jnp.bfloat16, jnp.float32
A0, B0, B1, A1, B2, A2, A3, B3 = range(0, 16, 2)
FG, BG, KX, KL, H0, H1 = range(16, 22)


def dot(a, b, ca, cb):
    return lax.dot_general(a, b, (((ca,), (cb,)), ((), ())), preferred_element_type=F32)


def nn(a, b):
    return dot(a, b, 1, 0)


def nt(a, b):
    return dot(a, b, 1, 1)


def tn(a, b):
    return dot(a, b, 0, 0)


def hot(shape, where):
    row = lax.broadcasted_iota(jnp.int32, shape, 0)
    col = lax.broadcasted_iota(jnp.int32, shape, 1)
    return jnp.where(where(row, col), 1.0, 0.0).astype(BF)


def place0(r, c):
    return ((r >> 4) & 1) * 128 + (r & 15) * 8 + (r >> 5) == c


def turn0(r, c):
    return ((r >> 1) & 7) * 32 + (r & 1) * 16 + (r >> 4) == c


def place1(r, c):
    return ((r >> 3) & 1) * 128 + (r >> 4) * 8 + (r & 7) == c


def turn1(r, c):
    return ((r >> 1) & 15) * 16 + (r & 1) * 8 + (r >> 5) == c


def order1(r, c):
    return ((r >> 1) & 7) * 32 + (r >> 4) * 2 + (r & 1) == c


def flip(where):
    return lambda r, c: where(c, r)


def body(
    x_in, f_in, s_in, k_in, c_in,
    mixed_ref, igrad_ref, kgrad_ref, bgrad_ref, fgrad_ref,
    xs, cs, fs, sec, kin, xt, gate, total, gat, mgrad, near, kpad, kcol, st, s11, mgr, tables,
    a0s, a0r, b0s, b0r, b1s, b1r, a1s, a1r,
    b2s, b2r, a2s, a2r, a3s, a3r, b3s, b3r,
    h0s, h0r, h1s, h1r,
    kxs, kxr, kls, klr, fgo, fgs, fgr, bgo, bgs, bgr,
    ssem, rsem, isem,
):
    seq = lax.axis_index("seq")
    chan = lax.axis_index("chan")
    mx = lax.rem(seq, NX)
    ml = lax.div(seq, NX)
    ahead = lax.rem(seq + 1, SEQ)
    behind = lax.rem(seq + SEQ - 1, SEQ)

    def x_peer(d):
        other = lax.rem(mx + d, NX)
        return other, (ml * NX + other, chan)

    def l_peer(d):
        other = lax.rem(ml + d, NL)
        return other, (other * NX + mx, chan)

    def c_peer(d):
        other = lax.rem(chan + d, CHAN)
        return other, (seq, other)

    barrier = pltpu.get_barrier_semaphore()

    def greet(peer, count):
        def step(d, carry):
            pl.semaphore_signal(barrier, inc=1, device_id=peer(d)[1], device_id_type=MESH)
            return carry

        lax.fori_loop(1, count, step, 0)

    loads = [
        pltpu.make_async_copy(x_in, xs.at[:, pl.ds(0, CH), :], isem.at[0]),
        pltpu.make_async_copy(f_in, fs, isem.at[1]),
        pltpu.make_async_copy(c_in, cs.at[:, pl.ds(0, CH), :], isem.at[2]),
        pltpu.make_async_copy(k_in, kin, isem.at[3]),
        pltpu.make_async_copy(s_in, sec, isem.at[4]),
    ]
    for load in loads:
        load.start()
    greet(x_peer, NX)
    greet(l_peer, NL)
    greet(c_peer, CHAN)
    pl.semaphore_signal(barrier, inc=1, device_id=(ahead, chan), device_id_type=MESH)
    pl.semaphore_signal(barrier, inc=1, device_id=(behind, chan), device_id_type=MESH)

    def remote(src, dst, device, sem):
        return pltpu.make_async_remote_copy(
            src_ref=src, dst_ref=dst, send_sem=ssem.at[sem], recv_sem=rsem.at[sem],
            device_id=device, device_id_type=MESH,
        )

    def scatter(send, recv, mine, peer, count, sem):
        def step(i, carry):
            d = count // 2 + lax.div(i + 1, 2) * (2 * lax.rem(i, 2) - 1)
            other, device = peer(d)
            remote(send.at[other], recv.at[mine], device, sem).start()
            return carry

        lax.fori_loop(0, count - 1, step, 0)

    def keep(send, recv, mine):
        recv[mine] = send[mine]

    def spread(send, recv, mine, peer, count, sem):
        def step(i, carry):
            d = count // 2 + lax.div(i + 1, 2) * (2 * lax.rem(i, 2) - 1)
            remote(send, recv.at[mine], peer(d)[1], sem).start()
            return carry

        lax.fori_loop(0, count - 1, step, 0)
        recv[mine] = send[...]

    def arrive(recv, count, sem):
        part = recv.at[pl.ds(0, count - 1)]
        pltpu.make_async_copy(part, part, rsem.at[sem]).wait()

    def sent(send, count, sem):
        part = send.at[pl.ds(0, count - 1)]
        pltpu.make_async_copy(part, part, ssem.at[sem]).wait()

    def flat(ref, b):
        return ref[b].reshape(256, ROWS)

    def over_x(value, send, recv, b, sem):
        send[b] = value.astype(BF).reshape(NX, 32, ROWS)
        scatter(send.at[b], recv.at[b], mx, x_peer, NX, sem + b)
        keep(send.at[b], recv.at[b], mx)

    def over_l(value, send, recv, b, sem):
        send[b] = value.astype(BF).reshape(NL, 16, ROWS)
        scatter(send.at[b], recv.at[b], ml, l_peer, NL, sem + b)
        keep(send.at[b], recv.at[b], ml)

    zero_rows = jnp.zeros((BATCH, ROWS - CH, EXT), BF)
    xs[:, CH:ROWS, :] = zero_rows
    cs[:, CH:ROWS, :] = zero_rows
    kpad[...] = jnp.zeros_like(kpad)
    tables[0] = hot((256, 256), place0)
    tables[1] = hot((256, 256), place1)
    shift1 = hot((EXT, EXT), lambda r, c: r == c + 1)
    shift2 = hot((EXT, EXT), lambda r, c: r == c + 2)

    loads[0].wait()
    loads[1].wait()
    p0 = tables[0]
    for b in range(BATCH):
        m0 = nn(xs[b, :, 0:BLK], fs[0]).astype(BF)
        m1 = nn(xs[b, :, BLK:EXT], fs[1]).astype(BF)
        a0s[b] = (nt(p0[:, 0:BLK], m0) + nt(p0[:, BLK:EXT], m1)).astype(BF).reshape(NX, 32, ROWS)
    loads[2].wait()
    head = hot((16, EXT), lambda r, c: (r == c) & (r < 2))
    for b in range(BATCH):
        h0s[b] = nt(head, cs[b]).astype(BF)

    pl.semaphore_wait(barrier, NX - 1 + NL - 1 + CHAN - 1 + 2)

    halo0 = remote(h0s, h0r, (behind, chan), H0)
    halo0.start()
    for b in range(BATCH):
        scatter(a0s.at[b], a0r.at[b], mx, x_peer, NX, A0 + b)
        keep(a0s.at[b], a0r.at[b], mx)

    loads[3].wait()
    kpad[0:3, 0:CH] = kin[...]
    kcol[0:128, :] = kpad[:, 0:128].T
    kcol[128:256, :] = kpad[:, 128:256].T

    def gate_from(lanes, b, cot, near1, near2):
        near[0, b, :, lanes] = near1.astype(BF)
        near[1, b, :, lanes] = near2.astype(BF)
        value = kcol[:, 0:1] * cot.astype(F32) + kcol[:, 1:2] * near1 + kcol[:, 2:3] * near2
        gate[b, :, lanes] = value
        mgrad[b, :, lanes] = (value * xs[b, :, lanes].astype(F32)).astype(BF)

    last = NL - 1
    p1 = tables[1]
    for b in range(BATCH):
        gate_from(slice(0, EXT), b, cs[b], nn(cs[b], shift1), nn(cs[b], shift2))
        b1s[b] = nt(p1, mgrad[b]).astype(BF).reshape(NL, 16, ROWS)

        def step(i, carry):
            other, device = l_peer(NL // 2 + lax.div(i + 1, 2) * (2 * lax.rem(i, 2) - 1))

            @pl.when(other != last)
            def _():
                remote(b1s.at[b, other], b1r.at[b, ml], device, B1 + b).start()

            return carry

        lax.fori_loop(0, NL - 1, step, 0)

    halo0.wait_recv()
    inside = (seq < SEQ - 1).astype(F32)
    high = slice(BLK, EXT)
    for b in range(BATCH):
        tail = (h0r[b].astype(F32) * inside).astype(BF)
        near1 = near[0, b, :, high].astype(F32)
        near2 = near[1, b, :, high].astype(F32)
        near1 = near1 + tn(tail, hot((16, BLK), lambda r, c: (r == 0) & (c == BLK - 1)))
        near2 = near2 + tn(tail, hot((16, BLK), lambda r, c: (r < 2) & (c == BLK - 2 + r)))
        gate_from(high, b, cs[b, :, high], near1, near2)
        b1s[b, last] = nt(tables[1, 16 * last : 16 * NL], mgrad[b]).astype(BF)

        @pl.when(ml != last)
        def _():
            remote(b1s.at[b, last], b1r.at[b, ml], (last * NX + mx, chan), B1 + b).start()

        keep(b1s.at[b], b1r.at[b], ml)

    tables[2] = hot((256, 256), turn0)
    tables[3] = hot((256, 256), flip(turn0))
    tables[4] = hot((256, 256), turn1)
    tables[5] = hot((256, 256), flip(turn1))
    tables[6] = hot((256, 256), order1)
    loads[4].wait()
    eye = hot((256, 256), lambda r, c: r == c)
    second = sec[0]
    st[...] = nt(eye, second).astype(BF)
    back = hot((256, 256), flip(order1))
    s11[...] = nt(nn(back, second).astype(BF), back).astype(BF)

    for b in range(BATCH):
        arrive(a0r.at[b], NX, A0 + b)
        over_l(nn(tables[2], flat(a0r, b)), b0s, b0r, b, B0)
    for b in range(BATCH):
        arrive(b1r.at[b], NL, B1 + b)
        over_x(nn(tables[4], flat(b1r, b)), a1s, a1r, b, A1)
    for b in range(BATCH):
        arrive(a1r.at[b], NX, A1 + b)
        over_x(nn(s11[...], flat(a1r, b)), a3s, a3r, b, A3)
        arrive(b0r.at[b], NL, B0 + b)
        over_l(nn(st[...], flat(b0r, b)), b2s, b2r, b, B2)
    for b in range(BATCH):
        arrive(a3r.at[b], NX, A3 + b)
        over_l(nn(tables[5], flat(a3r, b)), b3s, b3r, b, B3)
    grad = jnp.zeros((256, 256), F32)
    for b in range(BATCH):
        nat = nn(tables[6], flat(a1r, b)).astype(BF)
        grad = grad + nt(flat(b0r, b), nat)
    fgo[...] = grad.reshape(CHAN, 64, 256)
    fgs[...] = grad.astype(BF).reshape(CHAN, 64, 256)
    scatter(fgs, fgr, chan, c_peer, CHAN, FG)
    for b in range(BATCH):
        xt[b] = nt(eye, xs[b]).astype(BF)
    for b in range(BATCH):
        arrive(b2r.at[b], NL, B2 + b)
        over_x(nn(tables[3], flat(b2r, b)), a2s, a2r, b, A2)

    edge = hot((16, EXT), lambda r, c: (r < 2) & (c == EXT - 2 + r))
    prods = [jnp.zeros((ROWS, BLK), F32)] * 3
    for b in range(BATCH):
        arrive(a2r.at[b], NX, A2 + b)
        monarch = tn(flat(a2r, b), tables[0])
        gated = (xs[b].astype(F32) * monarch).astype(BF)
        gat[b] = gated
        h1s[b] = nt(edge, gated).astype(BF)
        gate[b] = gate[b] * monarch
        gated32 = gated.astype(F32)
        for j in range(3):
            window = cs[b] if j == 0 else near[j - 1, b]
            prod = gated32 * window.astype(F32)
            prods[j] = prods[j] + (prod[:, 0:BLK] + prod[:, BLK:EXT])
    halo1 = remote(h1s, h1r, (ahead, chan), H1)
    halo1.start()
    sums = [jnp.sum(prod, axis=1, keepdims=True) for prod in prods]
    lane = lax.broadcasted_iota(jnp.int32, (ROWS, 128), 1)
    wide = jnp.where(lane == 0, sums[0], jnp.where(lane == 1, sums[1], sums[2]))
    kxs[:, 0:128] = wide[0:128].T[0:8]
    kxs[:, 128:256] = wide[128:256].T[0:8]
    spread(kxs, kxr, mx, x_peer, NX, KX)

    far1 = hot((EXT, EXT), lambda r, c: r + 1 == c)
    far2 = hot((EXT, EXT), lambda r, c: r + 2 == c)
    for b in range(BATCH):
        total[b] = (
            kcol[:, 0:1] * gat[b].astype(F32)
            + kcol[:, 1:2] * nn(gat[b], far1)
            + kcol[:, 2:3] * nn(gat[b], far2)
        )

    for b in range(BATCH):
        arrive(b3r.at[b], NL, B3 + b)
        mgr[b] = tn(flat(b3r, b), tables[1]).astype(BF)
    for q in range(2):
        lanes = slice(q * BLK, (q + 1) * BLK)
        part = nn(xt[0, lanes, :], mgr[0, :, lanes]) + nn(xt[1, lanes, :], mgr[1, :, lanes])
        part = part.reshape(CHAN, 32, BLK)
        for o in range(CHAN):
            bgo[o, q] = part[o]
            bgs[o, q] = part[o].astype(BF)
    scatter(bgs, bgr, chan, c_peer, CHAN, BG)

    arrive(kxr, NX, KX)
    kls[...] = sum((kxr[i] for i in range(1, NX)), kxr[0])
    spread(kls, klr, ml, l_peer, NL, KL)

    for q in range(2):
        lanes = slice(q * BLK, (q + 1) * BLK)
        for b in range(BATCH):
            through = nt(mgr[b, :, lanes], fs[q])
            igrad_ref[b, :, lanes] = (gate[b, :, lanes] + through)[0:CH].astype(BF)

    halo1.wait_recv()
    inside = (seq > 0).astype(F32)
    mixed_ref[:, :, high] = total[:, 0:CH, high].astype(BF)
    for b in range(BATCH):
        prior = (h1r[b].astype(F32) * inside).astype(BF)
        edge1 = tn(prior, hot((16, BLK), lambda r, c: (r == 1) & (c == 0)))
        edge2 = tn(prior, hot((16, BLK), lambda r, c: (r < 2) & (r == c)))
        value = total[b, :, 0:BLK] + (kcol[:, 1:2] * edge1 + kcol[:, 2:3] * edge2)
        mixed_ref[b, :, 0:BLK] = value[0:CH].astype(BF)

    arrive(fgr, CHAN, FG)
    fgr[chan] = jnp.zeros((64, 256), BF)
    got = [fgr[i].astype(F32) for i in range(CHAN)]
    fgrad_ref[0] = fgo[chan] + ((got[0] + got[1]) + (got[2] + got[3]))
    arrive(bgr, CHAN, BG)
    bgr[chan] = jnp.zeros((2, 32, BLK), BF)
    got = [bgr[i].astype(F32) for i in range(CHAN)]
    bgrad_ref[...] = bgo[chan] + ((got[0] + got[1]) + (got[2] + got[3]))
    arrive(klr, NL, KL)
    whole = sum((klr[i] for i in range(1, NL)), klr[0])
    kgrad_ref[...] = whole[0:3, 0:CH]

    halo0.wait_send()
    halo1.wait_send()
    for b in range(BATCH):
        for send, sem in ((a0s, A0), (a1s, A1), (a2s, A2), (a3s, A3)):
            sent(send.at[b], NX, sem + b)
        for send, sem in ((b0s, B0), (b1s, B1), (b2s, B2), (b3s, B3)):
            sent(send.at[b], NL, sem + b)
    sent(fgs, CHAN, FG)
    sent(bgs, CHAN, BG)
    sent(kxr, NX, KX)
    sent(klr, NL, KL)


def emit(*refs):
    count = (len(refs) - 1) // 2
    sem = refs[-1]
    copies = [pltpu.make_async_copy(refs[i], refs[count + i], sem.at[i]) for i in range(count)]
    for copy in copies:
        copy.start()
    for copy in copies:
        copy.wait()


def shards(inputs, first_blocks, second_blocks, kernel, cotangent):
    vmem = pl.BlockSpec(memory_space=pltpu.VMEM)
    free = pl.BlockSpec(memory_space=pl.ANY)
    xbuf = pltpu.VMEM((BATCH, NX, 32, ROWS), BF)
    lbuf = pltpu.VMEM((BATCH, NL, 16, ROWS), BF)
    halo = pltpu.VMEM((BATCH, 16, ROWS), BF)
    plane = pltpu.VMEM((BATCH, ROWS, EXT), BF)
    square = pltpu.VMEM((256, 256), BF)
    shapes = (
        jax.ShapeDtypeStruct((BATCH, CH, EXT), BF),
        jax.ShapeDtypeStruct((BATCH, CH, EXT), BF),
        jax.ShapeDtypeStruct((3, CH), F32),
        jax.ShapeDtypeStruct((2, BLK // CHAN, BLK), F32),
        jax.ShapeDtypeStruct((1, 256 // CHAN, 256), F32),
    )
    results = pl.pallas_call(
        body,
        out_shape=shapes,
        in_specs=[free] * 5,
        out_specs=(vmem,) * 5,
        scratch_shapes=[
            plane, plane,
            pltpu.VMEM((2, BLK, BLK), BF), pltpu.VMEM((1, 256, 256), BF),
            pltpu.VMEM((3, CH), F32), plane,
            pltpu.VMEM((BATCH, ROWS, EXT), F32), pltpu.VMEM((BATCH, ROWS, EXT), F32),
            plane, plane,
            pltpu.VMEM((2, BATCH, ROWS, EXT), BF),
            pltpu.VMEM((128, 256), F32), pltpu.VMEM((ROWS, 128), F32),
            square, square, plane,
            pltpu.VMEM((7, 256, 256), BF),
            xbuf, xbuf, lbuf, lbuf, lbuf, lbuf, xbuf, xbuf,
            lbuf, lbuf, xbuf, xbuf, xbuf, xbuf, lbuf, lbuf,
            halo, halo, halo, halo,
            pltpu.VMEM((8, 256), F32), pltpu.VMEM((NX, 8, 256), F32),
            pltpu.VMEM((8, 256), F32), pltpu.VMEM((NL, 8, 256), F32),
            pltpu.VMEM((CHAN, 64, 256), F32),
            pltpu.VMEM((CHAN, 64, 256), BF), pltpu.VMEM((CHAN, 64, 256), BF),
            pltpu.VMEM((CHAN, 2, 32, BLK), F32),
            pltpu.VMEM((CHAN, 2, 32, BLK), BF), pltpu.VMEM((CHAN, 2, 32, BLK), BF),
            pltpu.SemaphoreType.DMA((22,)),
            pltpu.SemaphoreType.DMA((22,)),
            pltpu.SemaphoreType.DMA((5,)),
        ],
        compiler_params=pltpu.CompilerParams(
            collective_id=0, has_side_effects=True, vmem_limit_bytes=60 * 1024 * 1024
        ),
    )(inputs, first_blocks, second_blocks, kernel, cotangent)
    return pl.pallas_call(
        emit,
        out_shape=shapes,
        in_specs=[free] * 5,
        out_specs=(free,) * 5,
        scratch_shapes=[pltpu.SemaphoreType.DMA((5,))],
        compiler_params=pltpu.CompilerParams(vmem_limit_bytes=60 * 1024 * 1024),
    )(*results)


def solution(mesh):
    placed = (
        P(None, "chan", "seq"),
        P("seq", None, None),
        P("seq", None, None),
        P(None, "chan"),
        P(None, "chan", "seq"),
    )
    return jax.shard_map(
        shards,
        mesh=mesh,
        in_specs=placed,
        out_specs=(
            P(None, "chan", "seq"),
            P(None, "chan", "seq"),
            P(None, "chan"),
            P("seq", "chan", None),
            P("seq", "chan", None),
        ),
        check_vma=False,
    )
```

time: 577 us -> 81.2 us (0.14)
  blocking collectives: 367 us -> 0 us
  waiting for transfers between devices: 162 us -> 0 us
  Pallas kernels: 0 us -> 79.2 us
  starting transfers between devices: 18.3 us -> 0 us
  between operations: 14.9 us -> 0.64 us
  local copies, waits for them, and re-layouts: 9.49 us -> 0 us
    psum x1 -> x0, blocking collectives: 313 us -> none  [shards(): kernel_grad = lax.psum(jnp.stack(kernel_rows), 'seq')]
    unnamed x3 -> x0, waiting for transfers between devices: 111 us -> none
    pallas_call x0 -> x2, Pallas kernels: none -> 79.2 us  [the longest x1 60.1 us: shards(): pl.pallas_call(body, out_shape=shapes, in_specs=[free] * 5, out_specs=(vm...]
    all_to_all x2 -> x0, blocking collectives: 53.9 us -> none  [the longest x1 30.4 us: shards(): lax.all_to_all(mixed_in, 'seq', split_axis=2, concat_axis=3, tiled=True)]
    reduce_scatter x1 -> x0, waiting for transfers between devices: 40.1 us -> none  [shards(): lax.psum_scatter(factor_term, 'chan', scatter_dimension=1, tiled=True)]
    all_to_all x2 -> x0, starting transfers between devices: 14.5 us -> none  [the longest x1 8.27 us: shards(): lax.all_to_all(factor_out, 'seq', split_axis=3, concat_axis=2, tiled=True)]
  transfers between devices with their start and end apart: 6 -> 0, of which waited for: 4 -> 0; matrix products, arithmetic and copies ran while one was open for 1% -> 0% of each run, Pallas kernels for 0% -> 0%
where the time goes in v2:
time: 81.2 us; the launch traced here: 79.9 us
  Pallas kernels  79.2 us (98%)
    pallas_call x1, Pallas kernels, shards(): pl.pallas_call(body, out_shape=shapes, in_specs=[free] * 5, out_specs=(vm...  60.1 us
    pallas_call x1, Pallas kernels, shards(): pl.pallas_call(emit, out_shape=shapes, in_specs=[free] * 5, out_specs=(fr...  19.1 us

profile of v2, /device:TPU:1, one launch (start us, length us, event | category | flops | bytes accessed | tf_op | source)
XLA Modules:
  0.0 79.9 jit_solution(722213504781970884)
XLA Ops:
  0.6 60.1 %shard_map.92 = (bf16[2,240,256]{2,1,0:T(8,128)(2,1)}, bf16[2,240,256]{2,1,0:T(8,128)(2,1)}, f32[3,240]{1,0:T(4,128)}, f32[2,32,128]{2,1,0:T(8,128)}, f32[1,64,256]{2,1,0:T(8,128)}) custom-call(bf16[2,240,256]{2,1,0:T(8,128)(2,1)} %x_in.1, bf16[2,128,128]{2,1,0:T(8,128)(2,1)} %f_in.1, bf16[1,256,256]{2,1,0:T(8,128)(2,1)} %s_in.1, f32[3,240]{1,0:T(4,128)} %k_in.1, ...), custom_call_target="tpu_custom_call" | custom-call | tf_op jit(solution)/shard_map/pallas_call | solution.py:394
  60.7 19.1 %shard_map.93 = (bf16[2,240,256]{2,1,0:T(8,128)(2,1)}, bf16[2,240,256]{2,1,0:T(8,128)(2,1)}, f32[3,240]{1,0:T(4,128)}, f32[2,32,128]{2,1,0:T(8,128)}, f32[1,64,256]{2,1,0:T(8,128)}) custom-call(bf16[2,240,256]{2,1,0:T(8,128)(2,1)} %get-tuple-element.10.refs_0_, bf16[2,240,256]{2,1,0:T(8,128)(2,1)} %get-tuple-element.11.refs_1_, ...), custom_call_target="tpu_custom_call" | custom-call | tf_op jit(solution)/shard_map/pallas_call | solution.py:426

commit v3 on v2

--- a/solution.py
+++ b/solution.py
@@ -220,6 +220,10 @@
 
         lax.fori_loop(0, NL - 1, step, 0)
 
+    tables[2] = hot((256, 256), turn0)
+    arrive(a0r.at[0], NX, A0)
+    over_l(nn(tables[2], flat(a0r, 0)), b0s, b0r, 0, B0)
+
     halo0.wait_recv()
     inside = (seq < SEQ - 1).astype(F32)
     high = slice(BLK, EXT)
@@ -238,7 +242,9 @@
 
         keep(b1s.at[b], b1r.at[b], ml)
 
-    tables[2] = hot((256, 256), turn0)
+    arrive(a0r.at[1], NX, A0 + 1)
+    over_l(nn(tables[2], flat(a0r, 1)), b0s, b0r, 1, B0)
+
     tables[3] = hot((256, 256), flip(turn0))
     tables[4] = hot((256, 256), turn1)
     tables[5] = hot((256, 256), flip(turn1))
@@ -251,31 +257,28 @@
     s11[...] = nt(nn(back, second).astype(BF), back).astype(BF)
 
     for b in range(BATCH):
-        arrive(a0r.at[b], NX, A0 + b)
-        over_l(nn(tables[2], flat(a0r, b)), b0s, b0r, b, B0)
+        xt[b] = nt(eye, xs[b]).astype(BF)
     for b in range(BATCH):
         arrive(b1r.at[b], NL, B1 + b)
         over_x(nn(tables[4], flat(b1r, b)), a1s, a1r, b, A1)
     for b in range(BATCH):
+        arrive(b0r.at[b], NL, B0 + b)
+        over_l(nn(st[...], flat(b0r, b)), b2s, b2r, b, B2)
+    for b in range(BATCH):
         arrive(a1r.at[b], NX, A1 + b)
         over_x(nn(s11[...], flat(a1r, b)), a3s, a3r, b, A3)
-        arrive(b0r.at[b], NL, B0 + b)
-        over_l(nn(st[...], flat(b0r, b)), b2s, b2r, b, B2)
-    for b in range(BATCH):
-        arrive(a3r.at[b], NX, A3 + b)
-        over_l(nn(tables[5], flat(a3r, b)), b3s, b3r, b, B3)
     grad = jnp.zeros((256, 256), F32)
     for b in range(BATCH):
         nat = nn(tables[6], flat(a1r, b)).astype(BF)
         grad = grad + nt(flat(b0r, b), nat)
     fgo[...] = grad.reshape(CHAN, 64, 256)
     fgs[...] = grad.astype(BF).reshape(CHAN, 64, 256)
-    scatter(fgs, fgr, chan, c_peer, CHAN, FG)
-    for b in range(BATCH):
-        xt[b] = nt(eye, xs[b]).astype(BF)
     for b in range(BATCH):
         arrive(b2r.at[b], NL, B2 + b)
         over_x(nn(tables[3], flat(b2r, b)), a2s, a2r, b, A2)
+        arrive(a3r.at[b], NX, A3 + b)
+        over_l(nn(tables[5], flat(a3r, b)), b3s, b3r, b, B3)
+    scatter(fgs, fgr, chan, c_peer, CHAN, FG)
 
     edge = hot((16, EXT), lambda r, c: (r < 2) & (c == EXT - 2 + r))
     prods = [jnp.zeros((ROWS, BLK), F32)] * 3
@@ -309,6 +312,10 @@
             + kcol[:, 2:3] * nn(gat[b], far2)
         )
 
+    arrive(kxr, NX, KX)
+    kls[...] = sum((kxr[i] for i in range(1, NX)), kxr[0])
+    spread(kls, klr, ml, l_peer, NL, KL)
+
     for b in range(BATCH):
         arrive(b3r.at[b], NL, B3 + b)
         mgr[b] = tn(flat(b3r, b), tables[1]).astype(BF)
@@ -320,10 +327,6 @@
             bgo[o, q] = part[o]
             bgs[o, q] = part[o].astype(BF)
     scatter(bgs, bgr, chan, c_peer, CHAN, BG)
-
-    arrive(kxr, NX, KX)
-    kls[...] = sum((kxr[i] for i in range(1, NX)), kxr[0])
-    spread(kls, klr, ml, l_peer, NL, KL)
 
     for q in range(2):
         lanes = slice(q * BLK, (q + 1) * BLK)
@@ -367,13 +370,16 @@
 
 
 def emit(*refs):
-    count = (len(refs) - 1) // 2
-    sem = refs[-1]
-    copies = [pltpu.make_async_copy(refs[i], refs[count + i], sem.at[i]) for i in range(count)]
-    for copy in copies:
-        copy.start()
-    for copy in copies:
-        copy.wait()
+    ins, outs, held, sem = refs[0:5], refs[5:10], refs[10:15], refs[15]
+    loads = [pltpu.make_async_copy(ins[i], held[i], sem.at[0, i]) for i in range(5)]
+    stores = [pltpu.make_async_copy(held[i], outs[i], sem.at[1, i]) for i in range(5)]
+    for load in loads:
+        load.start()
+    for load, store in zip(loads, stores):
+        load.wait()
+        store.start()
+    for store in stores:
+        store.wait()
 
 
 def shards(inputs, first_blocks, second_blocks, kernel, cotangent):
@@ -428,7 +434,8 @@
         out_shape=shapes,
         in_specs=[free] * 5,
         out_specs=(free,) * 5,
-        scratch_shapes=[pltpu.SemaphoreType.DMA((5,))],
+        scratch_shapes=[pltpu.VMEM(one.shape, one.dtype) for one in shapes]
+        + [pltpu.SemaphoreType.DMA((2, 5))],
         compiler_params=pltpu.CompilerParams(vmem_limit_bytes=60 * 1024 * 1024),
     )(*results)
 

time: 81.2 us -> 65.4 us (0.81); the launches traced: 79.9 us -> 65.2 us
  Pallas kernels: 79.2 us -> 64.6 us
    pallas_call x1, Pallas kernels: 19.1 us -> 1.88 us  [shards(): pl.pallas_call(emit, out_shape=shapes, in_specs=[free] * 5, out_specs=(fr...]
    pallas_call x1, Pallas kernels: 60.1 us -> 62.7 us  [shards(): pl.pallas_call(body, out_shape=shapes, in_specs=[free] * 5, out_specs=(vm...]
where the time goes in v3:
time: 65.4 us; the launch traced here: 65.2 us
  Pallas kernels  64.6 us (99%)
    pallas_call x1, Pallas kernels, shards(): pl.pallas_call(body, out_shape=shapes, in_specs=[free] * 5, out_specs=(vm...  62.7 us
    pallas_call x1, Pallas kernels, shards(): pl.pallas_call(emit, out_shape=shapes, in_specs=[free] * 5, out_specs=(fr...  1.88 us

profile of v3, /device:TPU:1, one launch (start us, length us, event | category | flops | bytes accessed | tf_op | source)
XLA Modules:
  0.0 65.2 jit_solution(7944860631146521760)
XLA Ops:
  0.6 62.7 %shard_map.92 = (bf16[2,240,256]{2,1,0:T(8,128)(2,1)}, bf16[2,240,256]{2,1,0:T(8,128)(2,1)}, f32[3,240]{1,0:T(4,128)}, f32[2,32,128]{2,1,0:T(8,128)}, f32[1,64,256]{2,1,0:T(8,128)}) custom-call(bf16[2,240,256]{2,1,0:T(8,128)(2,1)} %x_in.1, bf16[2,128,128]{2,1,0:T(8,128)(2,1)} %f_in.1, bf16[1,256,256]{2,1,0:T(8,128)(2,1)} %s_in.1, f32[3,240]{1,0:T(4,128)} %k_in.1, ...), custom_call_target="tpu_custom_call" | custom-call | tf_op jit(solution)/shard_map/pallas_call | solution.py:400
  63.4 1.9 %shard_map.93 = (bf16[2,240,256]{2,1,0:T(8,128)(2,1)}, bf16[2,240,256]{2,1,0:T(8,128)(2,1)}, f32[3,240]{1,0:T(4,128)}, f32[2,32,128]{2,1,0:T(8,128)}, f32[1,64,256]{2,1,0:T(8,128)}) custom-call(bf16[2,240,256]{2,1,0:T(8,128)(2,1)} %get-tuple-element.10.refs_0_, bf16[2,240,256]{2,1,0:T(8,128)(2,1)} %get-tuple-element.11.refs_1_, ...), custom_call_target="tpu_custom_call" | custom-call | tf_op jit(solution)/shard_map/pallas_call | solution.py:432

commit v4 on v3

--- a/solution.py
+++ b/solution.py
@@ -64,7 +64,7 @@
 def body(
     x_in, f_in, s_in, k_in, c_in,
     mixed_ref, igrad_ref, kgrad_ref, bgrad_ref, fgrad_ref,
-    xs, cs, fs, sec, kin, xt, gate, total, gat, mgrad, near, kpad, kcol, st, s11, mgr, tables,
+    xs, cs, fs, sec, kin, xt, gate, total, gat, mon, mgrad, near, kpad, kcol, st, s11, mgr, tables,
     a0s, a0r, b0s, b0r, b1s, b1r, a1s, a1r,
     b2s, b2r, a2s, a2r, a3s, a3r, b3s, b3r,
     h0s, h0r, h1s, h1r,
@@ -100,9 +100,9 @@
         lax.fori_loop(1, count, step, 0)
 
     loads = [
+        pltpu.make_async_copy(c_in, cs.at[:, pl.ds(0, CH), :], isem.at[2]),
         pltpu.make_async_copy(x_in, xs.at[:, pl.ds(0, CH), :], isem.at[0]),
         pltpu.make_async_copy(f_in, fs, isem.at[1]),
-        pltpu.make_async_copy(c_in, cs.at[:, pl.ds(0, CH), :], isem.at[2]),
         pltpu.make_async_copy(k_in, kin, isem.at[3]),
         pltpu.make_async_copy(s_in, sec, isem.at[4]),
     ]
@@ -172,24 +172,21 @@
     shift2 = hot((EXT, EXT), lambda r, c: r == c + 2)
 
     loads[0].wait()
+    head = hot((16, EXT), lambda r, c: (r == c) & (r < 2))
+    for b in range(BATCH):
+        h0s[b] = nt(head, cs[b]).astype(BF)
+
+    pl.semaphore_wait(barrier, NX - 1 + NL - 1 + CHAN - 1 + 2)
+    halo0 = remote(h0s, h0r, (behind, chan), H0)
+    halo0.start()
+
     loads[1].wait()
+    loads[2].wait()
     p0 = tables[0]
     for b in range(BATCH):
         m0 = nn(xs[b, :, 0:BLK], fs[0]).astype(BF)
         m1 = nn(xs[b, :, BLK:EXT], fs[1]).astype(BF)
-        a0s[b] = (nt(p0[:, 0:BLK], m0) + nt(p0[:, BLK:EXT], m1)).astype(BF).reshape(NX, 32, ROWS)
-    loads[2].wait()
-    head = hot((16, EXT), lambda r, c: (r == c) & (r < 2))
-    for b in range(BATCH):
-        h0s[b] = nt(head, cs[b]).astype(BF)
-
-    pl.semaphore_wait(barrier, NX - 1 + NL - 1 + CHAN - 1 + 2)
-
-    halo0 = remote(h0s, h0r, (behind, chan), H0)
-    halo0.start()
-    for b in range(BATCH):
-        scatter(a0s.at[b], a0r.at[b], mx, x_peer, NX, A0 + b)
-        keep(a0s.at[b], a0r.at[b], mx)
+        over_x(nt(p0[:, 0:BLK], m0) + nt(p0[:, BLK:EXT], m1), a0s, a0r, b, A0)
 
     loads[3].wait()
     kpad[0:3, 0:CH] = kin[...]
@@ -280,22 +277,18 @@
         over_l(nn(tables[5], flat(a3r, b)), b3s, b3r, b, B3)
     scatter(fgs, fgr, chan, c_peer, CHAN, FG)
 
-    edge = hot((16, EXT), lambda r, c: (r < 2) & (c == EXT - 2 + r))
     prods = [jnp.zeros((ROWS, BLK), F32)] * 3
     for b in range(BATCH):
         arrive(a2r.at[b], NX, A2 + b)
         monarch = tn(flat(a2r, b), tables[0])
+        mon[b] = monarch.astype(BF)
         gated = (xs[b].astype(F32) * monarch).astype(BF)
         gat[b] = gated
-        h1s[b] = nt(edge, gated).astype(BF)
-        gate[b] = gate[b] * monarch
         gated32 = gated.astype(F32)
         for j in range(3):
             window = cs[b] if j == 0 else near[j - 1, b]
             prod = gated32 * window.astype(F32)
             prods[j] = prods[j] + (prod[:, 0:BLK] + prod[:, BLK:EXT])
-    halo1 = remote(h1s, h1r, (ahead, chan), H1)
-    halo1.start()
     sums = [jnp.sum(prod, axis=1, keepdims=True) for prod in prods]
     lane = lax.broadcasted_iota(jnp.int32, (ROWS, 128), 1)
     wide = jnp.where(lane == 0, sums[0], jnp.where(lane == 1, sums[1], sums[2]))
@@ -303,18 +296,11 @@
     kxs[:, 128:256] = wide[128:256].T[0:8]
     spread(kxs, kxr, mx, x_peer, NX, KX)
 
-    far1 = hot((EXT, EXT), lambda r, c: r + 1 == c)
-    far2 = hot((EXT, EXT), lambda r, c: r + 2 == c)
-    for b in range(BATCH):
-        total[b] = (
-            kcol[:, 0:1] * gat[b].astype(F32)
-            + kcol[:, 1:2] * nn(gat[b], far1)
-            + kcol[:, 2:3] * nn(gat[b], far2)
-        )
-
-    arrive(kxr, NX, KX)
-    kls[...] = sum((kxr[i] for i in range(1, NX)), kxr[0])
-    spread(kls, klr, ml, l_peer, NL, KL)
+    edge = hot((16, EXT), lambda r, c: (r < 2) & (c == EXT - 2 + r))
+    for b in range(BATCH):
+        h1s[b] = nt(edge, gat[b]).astype(BF)
+    halo1 = remote(h1s, h1r, (ahead, chan), H1)
+    halo1.start()
 
     for b in range(BATCH):
         arrive(b3r.at[b], NL, B3 + b)
@@ -328,11 +314,24 @@
             bgs[o, q] = part[o].astype(BF)
     scatter(bgs, bgr, chan, c_peer, CHAN, BG)
 
+    arrive(kxr, NX, KX)
+    kls[...] = sum((kxr[i] for i in range(1, NX)), kxr[0])
+    spread(kls, klr, ml, l_peer, NL, KL)
+
+    far1 = hot((EXT, EXT), lambda r, c: r + 1 == c)
+    far2 = hot((EXT, EXT), lambda r, c: r + 2 == c)
+    for b in range(BATCH):
+        total[b] = (
+            kcol[:, 0:1] * gat[b].astype(F32)
+            + kcol[:, 1:2] * nn(gat[b], far1)
+            + kcol[:, 2:3] * nn(gat[b], far2)
+        )
     for q in range(2):
         lanes = slice(q * BLK, (q + 1) * BLK)
         for b in range(BATCH):
             through = nt(mgr[b, :, lanes], fs[q])
-            igrad_ref[b, :, lanes] = (gate[b, :, lanes] + through)[0:CH].astype(BF)
+            direct = gate[b, :, lanes] * mon[b, :, lanes].astype(F32)
+            igrad_ref[b, :, lanes] = (direct + through)[0:CH].astype(BF)
 
     halo1.wait_recv()
     inside = (seq > 0).astype(F32)
@@ -407,7 +406,7 @@
             pltpu.VMEM((2, BLK, BLK), BF), pltpu.VMEM((1, 256, 256), BF),
             pltpu.VMEM((3, CH), F32), plane,
             pltpu.VMEM((BATCH, ROWS, EXT), F32), pltpu.VMEM((BATCH, ROWS, EXT), F32),
-            plane, plane,
+            plane, plane, plane,
             pltpu.VMEM((2, BATCH, ROWS, EXT), BF),
             pltpu.VMEM((128, 256), F32), pltpu.VMEM((ROWS, 128), F32),
             square, square, plane,

time: 65.4 us -> 64.2 us (0.982)
  Pallas kernels: 64.6 us -> 63.4 us
    pallas_call x1, Pallas kernels: 62.7 us -> 61.6 us  [shards(): pl.pallas_call(body, out_shape=shapes, in_specs=[free] * 5, out_specs=(vm...]
where the time goes in v4:
time: 64.2 us; the launch traced here: 64.1 us
  Pallas kernels  63.4 us (99%)
    pallas_call x1, Pallas kernels, shards(): pl.pallas_call(body, out_shape=shapes, in_specs=[free] * 5, out_specs=(vm...  61.6 us
    pallas_call x1, Pallas kernels, shards(): pl.pallas_call(emit, out_shape=shapes, in_specs=[free] * 5, out_specs=(fr...  1.88 us

profile of v4, /device:TPU:1, one launch (start us, length us, event | category | flops | bytes accessed | tf_op | source)
XLA Modules:
  0.0 64.1 jit_solution(14179570330870887037)
XLA Ops:
  0.6 61.6 %shard_map.92 = (bf16[2,240,256]{2,1,0:T(8,128)(2,1)}, bf16[2,240,256]{2,1,0:T(8,128)(2,1)}, f32[3,240]{1,0:T(4,128)}, f32[2,32,128]{2,1,0:T(8,128)}, f32[1,64,256]{2,1,0:T(8,128)}) custom-call(bf16[2,240,256]{2,1,0:T(8,128)(2,1)} %x_in.1, bf16[2,128,128]{2,1,0:T(8,128)(2,1)} %f_in.1, bf16[1,256,256]{2,1,0:T(8,128)(2,1)} %s_in.1, f32[3,240]{1,0:T(4,128)} %k_in.1, ...), custom_call_target="tpu_custom_call" | custom-call | tf_op jit(solution)/shard_map/pallas_call | solution.py:399
  62.2 1.9 %shard_map.93 = (bf16[2,240,256]{2,1,0:T(8,128)(2,1)}, bf16[2,240,256]{2,1,0:T(8,128)(2,1)}, f32[3,240]{1,0:T(4,128)}, f32[2,32,128]{2,1,0:T(8,128)}, f32[1,64,256]{2,1,0:T(8,128)}) custom-call(bf16[2,240,256]{2,1,0:T(8,128)(2,1)} %get-tuple-element.10.refs_0_, bf16[2,240,256]{2,1,0:T(8,128)(2,1)} %get-tuple-element.11.refs_1_, ...), custom_call_target="tpu_custom_call" | custom-call | tf_op jit(solution)/shard_map/pallas_call | solution.py:431

commit v5 on v4

--- a/solution.py
+++ b/solution.py
@@ -63,13 +63,14 @@
 
 def body(
     x_in, f_in, s_in, k_in, c_in,
+    mixed_out, igrad_out, kgrad_out, bgrad_out, fgrad_out,
     mixed_ref, igrad_ref, kgrad_ref, bgrad_ref, fgrad_ref,
     xs, cs, fs, sec, kin, xt, gate, total, gat, mon, mgrad, near, kpad, kcol, st, s11, mgr, tables,
     a0s, a0r, b0s, b0r, b1s, b1r, a1s, a1r,
     b2s, b2r, a2s, a2r, a3s, a3r, b3s, b3r,
     h0s, h0r, h1s, h1r,
     kxs, kxr, kls, klr, fgo, fgs, fgr, bgo, bgs, bgr,
-    ssem, rsem, isem,
+    ssem, rsem, isem, osem,
 ):
     seq = lax.axis_index("seq")
     chan = lax.axis_index("chan")
@@ -108,8 +109,8 @@
     ]
     for load in loads:
         load.start()
+    greet(l_peer, NL)
     greet(x_peer, NX)
-    greet(l_peer, NL)
     greet(c_peer, CHAN)
     pl.semaphore_signal(barrier, inc=1, device_id=(ahead, chan), device_id_type=MESH)
     pl.semaphore_signal(barrier, inc=1, device_id=(behind, chan), device_id_type=MESH)
@@ -175,18 +176,14 @@
     head = hot((16, EXT), lambda r, c: (r == c) & (r < 2))
     for b in range(BATCH):
         h0s[b] = nt(head, cs[b]).astype(BF)
-
-    pl.semaphore_wait(barrier, NX - 1 + NL - 1 + CHAN - 1 + 2)
-    halo0 = remote(h0s, h0r, (behind, chan), H0)
-    halo0.start()
-
     loads[1].wait()
     loads[2].wait()
     p0 = tables[0]
     for b in range(BATCH):
         m0 = nn(xs[b, :, 0:BLK], fs[0]).astype(BF)
         m1 = nn(xs[b, :, BLK:EXT], fs[1]).astype(BF)
-        over_x(nt(p0[:, 0:BLK], m0) + nt(p0[:, BLK:EXT], m1), a0s, a0r, b, A0)
+        rows = nt(p0[:, 0:BLK], m0) + nt(p0[:, BLK:EXT], m1)
+        a0s[b] = rows.astype(BF).reshape(NX, 32, ROWS)
 
     loads[3].wait()
     kpad[0:3, 0:CH] = kin[...]
@@ -206,6 +203,14 @@
         gate_from(slice(0, EXT), b, cs[b], nn(cs[b], shift1), nn(cs[b], shift2))
         b1s[b] = nt(p1, mgrad[b]).astype(BF).reshape(NL, 16, ROWS)
 
+    pl.semaphore_wait(barrier, NX - 1 + NL - 1 + CHAN - 1 + 2)
+
+    halo0 = remote(h0s, h0r, (behind, chan), H0)
+    halo0.start()
+    for b in range(BATCH):
+        scatter(a0s.at[b], a0r.at[b], mx, x_peer, NX, A0 + b)
+    for b in range(BATCH):
+
         def step(i, carry):
             other, device = l_peer(NL // 2 + lax.div(i + 1, 2) * (2 * lax.rem(i, 2) - 1))
 
@@ -216,32 +221,10 @@
             return carry
 
         lax.fori_loop(0, NL - 1, step, 0)
+    for b in range(BATCH):
+        keep(a0s.at[b], a0r.at[b], mx)
 
     tables[2] = hot((256, 256), turn0)
-    arrive(a0r.at[0], NX, A0)
-    over_l(nn(tables[2], flat(a0r, 0)), b0s, b0r, 0, B0)
-
-    halo0.wait_recv()
-    inside = (seq < SEQ - 1).astype(F32)
-    high = slice(BLK, EXT)
-    for b in range(BATCH):
-        tail = (h0r[b].astype(F32) * inside).astype(BF)
-        near1 = near[0, b, :, high].astype(F32)
-        near2 = near[1, b, :, high].astype(F32)
-        near1 = near1 + tn(tail, hot((16, BLK), lambda r, c: (r == 0) & (c == BLK - 1)))
-        near2 = near2 + tn(tail, hot((16, BLK), lambda r, c: (r < 2) & (c == BLK - 2 + r)))
-        gate_from(high, b, cs[b, :, high], near1, near2)
-        b1s[b, last] = nt(tables[1, 16 * last : 16 * NL], mgrad[b]).astype(BF)
-
-        @pl.when(ml != last)
-        def _():
-            remote(b1s.at[b, last], b1r.at[b, ml], (last * NX + mx, chan), B1 + b).start()
-
-        keep(b1s.at[b], b1r.at[b], ml)
-
-    arrive(a0r.at[1], NX, A0 + 1)
-    over_l(nn(tables[2], flat(a0r, 1)), b0s, b0r, 1, B0)
-
     tables[3] = hot((256, 256), flip(turn0))
     tables[4] = hot((256, 256), turn1)
     tables[5] = hot((256, 256), flip(turn1))
@@ -252,6 +235,30 @@
     st[...] = nt(eye, second).astype(BF)
     back = hot((256, 256), flip(order1))
     s11[...] = nt(nn(back, second).astype(BF), back).astype(BF)
+
+    arrive(a0r.at[0], NX, A0)
+    over_l(nn(tables[2], flat(a0r, 0)), b0s, b0r, 0, B0)
+
+    halo0.wait_recv()
+    inside = (seq < SEQ - 1).astype(F32)
+    high = slice(BLK, EXT)
+    for b in range(BATCH):
+        tail = (h0r[b].astype(F32) * inside).astype(BF)
+        near1 = near[0, b, :, high].astype(F32)
+        near2 = near[1, b, :, high].astype(F32)
+        near1 = near1 + tn(tail, hot((16, BLK), lambda r, c: (r == 0) & (c == BLK - 1)))
+        near2 = near2 + tn(tail, hot((16, BLK), lambda r, c: (r < 2) & (c == BLK - 2 + r)))
+        gate_from(high, b, cs[b, :, high], near1, near2)
+        b1s[b, last] = nt(tables[1, 16 * last : 16 * NL], mgrad[b]).astype(BF)
+
+        @pl.when(ml != last)
+        def _():
+            remote(b1s.at[b, last], b1r.at[b, ml], (last * NX + mx, chan), B1 + b).start()
+
+        keep(b1s.at[b], b1r.at[b], ml)
+
+    arrive(a0r.at[1], NX, A0 + 1)
+    over_l(nn(tables[2], flat(a0r, 1)), b0s, b0r, 1, B0)
 
     for b in range(BATCH):
         xt[b] = nt(eye, xs[b]).astype(BF)
@@ -333,6 +340,15 @@
             direct = gate[b, :, lanes] * mon[b, :, lanes].astype(F32)
             igrad_ref[b, :, lanes] = (direct + through)[0:CH].astype(BF)
 
+    stores = [
+        pltpu.make_async_copy(igrad_ref, igrad_out, osem.at[0]),
+        pltpu.make_async_copy(mixed_ref, mixed_out, osem.at[1]),
+        pltpu.make_async_copy(fgrad_ref, fgrad_out, osem.at[2]),
+        pltpu.make_async_copy(bgrad_ref, bgrad_out, osem.at[3]),
+        pltpu.make_async_copy(kgrad_ref, kgrad_out, osem.at[4]),
+    ]
+    stores[0].start()
+
     halo1.wait_recv()
     inside = (seq > 0).astype(F32)
     mixed_ref[:, :, high] = total[:, 0:CH, high].astype(BF)
@@ -342,18 +358,22 @@
         edge2 = tn(prior, hot((16, BLK), lambda r, c: (r < 2) & (r == c)))
         value = total[b, :, 0:BLK] + (kcol[:, 1:2] * edge1 + kcol[:, 2:3] * edge2)
         mixed_ref[b, :, 0:BLK] = value[0:CH].astype(BF)
+    stores[1].start()
 
     arrive(fgr, CHAN, FG)
     fgr[chan] = jnp.zeros((64, 256), BF)
     got = [fgr[i].astype(F32) for i in range(CHAN)]
     fgrad_ref[0] = fgo[chan] + ((got[0] + got[1]) + (got[2] + got[3]))
+    stores[2].start()
     arrive(bgr, CHAN, BG)
     bgr[chan] = jnp.zeros((2, 32, BLK), BF)
     got = [bgr[i].astype(F32) for i in range(CHAN)]
     bgrad_ref[...] = bgo[chan] + ((got[0] + got[1]) + (got[2] + got[3]))
+    stores[3].start()
     arrive(klr, NL, KL)
     whole = sum((klr[i] for i in range(1, NL)), klr[0])
     kgrad_ref[...] = whole[0:3, 0:CH]
+    stores[4].start()
 
     halo0.wait_send()
     halo1.wait_send()
@@ -366,6 +386,8 @@
     sent(bgs, CHAN, BG)
     sent(kxr, NX, KX)
     sent(klr, NL, KL)
+    for store in stores:
+        store.wait()
 
 
 def emit(*refs):
@@ -382,7 +404,6 @@
 
 
 def shards(inputs, first_blocks, second_blocks, kernel, cotangent):
-    vmem = pl.BlockSpec(memory_space=pltpu.VMEM)
     free = pl.BlockSpec(memory_space=pl.ANY)
     xbuf = pltpu.VMEM((BATCH, NX, 32, ROWS), BF)
     lbuf = pltpu.VMEM((BATCH, NL, 16, ROWS), BF)
@@ -400,8 +421,9 @@
         body,
         out_shape=shapes,
         in_specs=[free] * 5,
-        out_specs=(vmem,) * 5,
-        scratch_shapes=[
+        out_specs=(free,) * 5,
+        scratch_shapes=[pltpu.VMEM(one.shape, one.dtype) for one in shapes]
+        + [
             plane, plane,
             pltpu.VMEM((2, BLK, BLK), BF), pltpu.VMEM((1, 256, 256), BF),
             pltpu.VMEM((3, CH), F32), plane,
@@ -423,6 +445,7 @@
             pltpu.SemaphoreType.DMA((22,)),
             pltpu.SemaphoreType.DMA((22,)),
             pltpu.SemaphoreType.DMA((5,)),
+            pltpu.SemaphoreType.DMA((5,)),
         ],
         compiler_params=pltpu.CompilerParams(
             collective_id=0, has_side_effects=True, vmem_limit_bytes=60 * 1024 * 1024

time: 64.2 us -> 63.4 us (0.988)
  the two profiles are of different devices: /device:TPU:1 before, /device:TPU:8 now
where the time goes in v5:
time: 63.4 us; the launch traced here: 63.2 us
  Pallas kernels  62.6 us (99%)
  between operations  0.64 us (1%)
    pallas_call x1, Pallas kernels, shards(): pl.pallas_call(body, out_shape=shapes, in_specs=[free] * 5, out_specs=(fr...  60.7 us
    pallas_call x1, Pallas kernels, shards(): pl.pallas_call(emit, out_shape=shapes, in_specs=[free] * 5, out_specs=(fr...  1.88 us

profile of v5, /device:TPU:8, one launch (start us, length us, event | category | flops | bytes accessed | tf_op | source)
XLA Modules:
  0.0 63.2 jit_solution(7432893608538208103)
XLA Ops:
  0.6 60.7 %shard_map.92 = (bf16[2,240,256]{2,1,0:T(8,128)(2,1)}, bf16[2,240,256]{2,1,0:T(8,128)(2,1)}, f32[3,240]{1,0:T(4,128)}, f32[2,32,128]{2,1,0:T(8,128)}, f32[1,64,256]{2,1,0:T(8,128)}) custom-call(bf16[2,240,256]{2,1,0:T(8,128)(2,1)} %x_in.1, bf16[2,128,128]{2,1,0:T(8,128)(2,1)} %f_in.1, bf16[1,256,256]{2,1,0:T(8,128)(2,1)} %s_in.1, f32[3,240]{1,0:T(4,128)} %k_in.1, ...), custom_call_target="tpu_custom_call" | custom-call | tf_op jit(solution)/shard_map/pallas_call | solution.py:420
  61.4 1.9 %shard_map.93 = (bf16[2,240,256]{2,1,0:T(8,128)(2,1)}, bf16[2,240,256]{2,1,0:T(8,128)(2,1)}, f32[3,240]{1,0:T(4,128)}, f32[2,32,128]{2,1,0:T(8,128)}, f32[1,64,256]{2,1,0:T(8,128)}) custom-call(bf16[2,240,256]{2,1,0:T(8,128)(2,1)} %get-tuple-element.10.refs_0_, bf16[2,240,256]{2,1,0:T(8,128)(2,1)} %get-tuple-element.11.refs_1_, ...), custom_call_target="tpu_custom_call" | custom-call | tf_op jit(solution)/shard_map/pallas_call | solution.py:454

commit v6 on v5

--- a/solution.py
+++ b/solution.py
@@ -12,7 +12,7 @@
 MESH = pl.DeviceIdType.MESH
 BF, F32 = jnp.bfloat16, jnp.float32
 A0, B0, B1, A1, B2, A2, A3, B3 = range(0, 16, 2)
-FG, BG, KX, KL, H0, H1 = range(16, 22)
+FG, FH, BG, KX, KL, H0, H1 = range(16, 23)
 
 
 def dot(a, b, ca, cb):
@@ -69,7 +69,7 @@
     a0s, a0r, b0s, b0r, b1s, b1r, a1s, a1r,
     b2s, b2r, a2s, a2r, a3s, a3r, b3s, b3r,
     h0s, h0r, h1s, h1r,
-    kxs, kxr, kls, klr, fgo, fgs, fgr, bgo, bgs, bgr,
+    kxs, kxr, kls, klr, fgo, fgp, fgs, fgr, bgo, bgs, bgr,
     ssem, rsem, isem, osem,
 ):
     seq = lax.axis_index("seq")
@@ -276,13 +276,19 @@
         nat = nn(tables[6], flat(a1r, b)).astype(BF)
         grad = grad + nt(flat(b0r, b), nat)
     fgo[...] = grad.reshape(CHAN, 64, 256)
-    fgs[...] = grad.astype(BF).reshape(CHAN, 64, 256)
+    core = lax.rem(chan, 2)
+    half = lax.div(chan, 2)
+    for h in range(2):
+        remote(fgo.at[2 * h + 1 - core], fgp.at[h], (seq, 2 * half + 1 - core), FG).start()
     for b in range(BATCH):
         arrive(b2r.at[b], NL, B2 + b)
         over_x(nn(tables[3], flat(b2r, b)), a2s, a2r, b, A2)
         arrive(a3r.at[b], NX, A3 + b)
         over_l(nn(tables[5], flat(a3r, b)), b3s, b3r, b, B3)
-    scatter(fgs, fgr, chan, c_peer, CHAN, FG)
+    pltpu.make_async_copy(fgp, fgp, rsem.at[FG]).wait()
+    fgs[...] = (fgo[2 * (1 - half) + core] + fgp[1 - half]).astype(BF)
+    pair = remote(fgs, fgr, (seq, 2 * (1 - half) + core), FH)
+    pair.start()
 
     prods = [jnp.zeros((ROWS, BLK), F32)] * 3
     for b in range(BATCH):
@@ -360,10 +366,8 @@
         mixed_ref[b, :, 0:BLK] = value[0:CH].astype(BF)
     stores[1].start()
 
-    arrive(fgr, CHAN, FG)
-    fgr[chan] = jnp.zeros((64, 256), BF)
-    got = [fgr[i].astype(F32) for i in range(CHAN)]
-    fgrad_ref[0] = fgo[chan] + ((got[0] + got[1]) + (got[2] + got[3]))
+    pair.wait_recv()
+    fgrad_ref[0] = (fgo[chan] + fgp[half]) + fgr[...].astype(F32)
     stores[2].start()
     arrive(bgr, CHAN, BG)
     bgr[chan] = jnp.zeros((2, 32, BLK), BF)
@@ -382,7 +386,8 @@
             sent(send.at[b], NX, sem + b)
         for send, sem in ((b0s, B0), (b1s, B1), (b2s, B2), (b3s, B3)):
             sent(send.at[b], NL, sem + b)
-    sent(fgs, CHAN, FG)
+    pltpu.make_async_copy(fgp, fgp, ssem.at[FG]).wait()
+    pair.wait_send()
     sent(bgs, CHAN, BG)
     sent(kxr, NX, KX)
     sent(klr, NL, KL)
@@ -392,8 +397,16 @@
 
 def emit(*refs):
     ins, outs, held, sem = refs[0:5], refs[5:10], refs[10:15], refs[15]
-    loads = [pltpu.make_async_copy(ins[i], held[i], sem.at[0, i]) for i in range(5)]
-    stores = [pltpu.make_async_copy(held[i], outs[i], sem.at[1, i]) for i in range(5)]
+    parts = [(0, 0), (1, 0), (0, 1), (1, 1), (4, 0), (3, 0), (2, 0)]
+
+    def piece(ref, i, b):
+        return ref.at[b] if i < 2 else ref
+
+    loads, stores = [], []
+    for n, (i, b) in enumerate(parts):
+        source, stage, target = piece(ins[i], i, b), piece(held[i], i, b), piece(outs[i], i, b)
+        loads.append(pltpu.make_async_copy(source, stage, sem.at[0, n]))
+        stores.append(pltpu.make_async_copy(stage, target, sem.at[1, n]))
     for load in loads:
         load.start()
     for load, store in zip(loads, stores):
@@ -439,11 +452,11 @@
             pltpu.VMEM((8, 256), F32), pltpu.VMEM((NX, 8, 256), F32),
             pltpu.VMEM((8, 256), F32), pltpu.VMEM((NL, 8, 256), F32),
             pltpu.VMEM((CHAN, 64, 256), F32),
-            pltpu.VMEM((CHAN, 64, 256), BF), pltpu.VMEM((CHAN, 64, 256), BF),
+            pltpu.VMEM((2, 64, 256), F32), pltpu.VMEM((64, 256), BF), pltpu.VMEM((64, 256), BF),
             pltpu.VMEM((CHAN, 2, 32, BLK), F32),
             pltpu.VMEM((CHAN, 2, 32, BLK), BF), pltpu.VMEM((CHAN, 2, 32, BLK), BF),
-            pltpu.SemaphoreType.DMA((22,)),
-            pltpu.SemaphoreType.DMA((22,)),
+            pltpu.SemaphoreType.DMA((23,)),
+            pltpu.SemaphoreType.DMA((23,)),
             pltpu.SemaphoreType.DMA((5,)),
             pltpu.SemaphoreType.DMA((5,)),
         ],
@@ -457,7 +470,7 @@
         in_specs=[free] * 5,
         out_specs=(free,) * 5,
         scratch_shapes=[pltpu.VMEM(one.shape, one.dtype) for one in shapes]
-        + [pltpu.SemaphoreType.DMA((2, 5))],
+        + [pltpu.SemaphoreType.DMA((2, 7))],
         compiler_params=pltpu.CompilerParams(vmem_limit_bytes=60 * 1024 * 1024),
     )(*results)
 

time: 63.4 us -> 61.9 us (0.976)
  Pallas kernels: 62.6 us -> 61.1 us
    pallas_call x1, Pallas kernels: 60.7 us -> 59.2 us  [shards(): pl.pallas_call(body, out_shape=shapes, in_specs=[free] * 5, out_specs=(fr...]
where the time goes in v6:
time: 61.9 us; the launch traced here: 61.8 us
  Pallas kernels  61.1 us (99%)
  between operations  0.64 us (1%)
    pallas_call x1, Pallas kernels, shards(): pl.pallas_call(body, out_shape=shapes, in_specs=[free] * 5, out_specs=(fr...  59.2 us
    pallas_call x1, Pallas kernels, shards(): pl.pallas_call(emit, out_shape=shapes, in_specs=[free] * 5, out_specs=(fr...  1.88 us

profile of v6, /device:TPU:8, one launch (start us, length us, event | category | flops | bytes accessed | tf_op | source)
XLA Modules:
  0.0 61.8 jit_solution(6826414798908512052)
XLA Ops:
  0.6 59.2 %shard_map.92 = (bf16[2,240,256]{2,1,0:T(8,128)(2,1)}, bf16[2,240,256]{2,1,0:T(8,128)(2,1)}, f32[3,240]{1,0:T(4,128)}, f32[2,32,128]{2,1,0:T(8,128)}, f32[1,64,256]{2,1,0:T(8,128)}) custom-call(bf16[2,240,256]{2,1,0:T(8,128)(2,1)} %x_in.1, bf16[2,128,128]{2,1,0:T(8,128)(2,1)} %f_in.1, bf16[1,256,256]{2,1,0:T(8,128)(2,1)} %s_in.1, f32[3,240]{1,0:T(4,128)} %k_in.1, ...), custom_call_target="tpu_custom_call" | custom-call | tf_op jit(solution)/shard_map/pallas_call | solution.py:433
  59.9 1.9 %shard_map.93 = (bf16[2,240,256]{2,1,0:T(8,128)(2,1)}, bf16[2,240,256]{2,1,0:T(8,128)(2,1)}, f32[3,240]{1,0:T(4,128)}, f32[2,32,128]{2,1,0:T(8,128)}, f32[1,64,256]{2,1,0:T(8,128)}) custom-call(bf16[2,240,256]{2,1,0:T(8,128)(2,1)} %get-tuple-element.10.refs_0_, bf16[2,240,256]{2,1,0:T(8,128)(2,1)} %get-tuple-element.11.refs_1_, ...), custom_call_target="tpu_custom_call" | custom-call | tf_op jit(solution)/shard_map/pallas_call | solution.py:467

commit v7 on v6

--- a/solution.py
+++ b/solution.py
@@ -285,10 +285,6 @@
         over_x(nn(tables[3], flat(b2r, b)), a2s, a2r, b, A2)
         arrive(a3r.at[b], NX, A3 + b)
         over_l(nn(tables[5], flat(a3r, b)), b3s, b3r, b, B3)
-    pltpu.make_async_copy(fgp, fgp, rsem.at[FG]).wait()
-    fgs[...] = (fgo[2 * (1 - half) + core] + fgp[1 - half]).astype(BF)
-    pair = remote(fgs, fgr, (seq, 2 * (1 - half) + core), FH)
-    pair.start()
 
     prods = [jnp.zeros((ROWS, BLK), F32)] * 3
     for b in range(BATCH):
@@ -303,10 +299,11 @@
             prod = gated32 * window.astype(F32)
             prods[j] = prods[j] + (prod[:, 0:BLK] + prod[:, BLK:EXT])
     sums = [jnp.sum(prod, axis=1, keepdims=True) for prod in prods]
-    lane = lax.broadcasted_iota(jnp.int32, (ROWS, 128), 1)
-    wide = jnp.where(lane == 0, sums[0], jnp.where(lane == 1, sums[1], sums[2]))
-    kxs[:, 0:128] = wide[0:128].T[0:8]
-    kxs[:, 128:256] = wide[128:256].T[0:8]
+    lane = lax.broadcasted_iota(jnp.int32, (128, 128), 1)
+    wide = jnp.zeros((128, 128), F32)
+    for j in range(3):
+        wide = jnp.where(lane == j, sums[j][0:128], jnp.where(lane == 3 + j, sums[j][128:256], wide))
+    kxs[...] = wide.T[0:8]
     spread(kxs, kxr, mx, x_peer, NX, KX)
 
     edge = hot((16, EXT), lambda r, c: (r < 2) & (c == EXT - 2 + r))
@@ -314,6 +311,10 @@
         h1s[b] = nt(edge, gat[b]).astype(BF)
     halo1 = remote(h1s, h1r, (ahead, chan), H1)
     halo1.start()
+    pltpu.make_async_copy(fgp, fgp, rsem.at[FG]).wait()
+    fgs[...] = (fgo[2 * (1 - half) + core] + fgp[1 - half]).astype(BF)
+    pair = remote(fgs, fgr, (seq, 2 * (1 - half) + core), FH)
+    pair.start()
 
     for b in range(BATCH):
         arrive(b3r.at[b], NL, B3 + b)
@@ -376,7 +377,8 @@
     stores[3].start()
     arrive(klr, NL, KL)
     whole = sum((klr[i] for i in range(1, NL)), klr[0])
-    kgrad_ref[...] = whole[0:3, 0:CH]
+    kgrad_ref[:, 0:128] = whole[0:3]
+    kgrad_ref[:, 128:CH] = whole[3:6, 0 : CH - 128]
     stores[4].start()
 
     halo0.wait_send()
@@ -449,8 +451,8 @@
             xbuf, xbuf, lbuf, lbuf, lbuf, lbuf, xbuf, xbuf,
             lbuf, lbuf, xbuf, xbuf, xbuf, xbuf, lbuf, lbuf,
             halo, halo, halo, halo,
-            pltpu.VMEM((8, 256), F32), pltpu.VMEM((NX, 8, 256), F32),
-            pltpu.VMEM((8, 256), F32), pltpu.VMEM((NL, 8, 256), F32),
+            pltpu.VMEM((8, 128), F32), pltpu.VMEM((NX, 8, 128), F32),
+            pltpu.VMEM((8, 128), F32), pltpu.VMEM((NL, 8, 128), F32),
             pltpu.VMEM((CHAN, 64, 256), F32),
             pltpu.VMEM((2, 64, 256), F32), pltpu.VMEM((64, 256), BF), pltpu.VMEM((64, 256), BF),
             pltpu.VMEM((CHAN, 2, 32, BLK), F32),

time: 61.9 us -> 61 us (0.985)
  Pallas kernels: 61.1 us -> 60.2 us
    pallas_call x1, Pallas kernels: 59.2 us -> 58.3 us  [shards(): pl.pallas_call(body, out_shape=shapes, in_specs=[free] * 5, out_specs=(fr...]
where the time goes in v7:
time: 61 us; the launch traced here: 60.9 us
  Pallas kernels  60.2 us (99%)
  between operations  0.64 us (1%)
    pallas_call x1, Pallas kernels, shards(): pl.pallas_call(body, out_shape=shapes, in_specs=[free] * 5, out_specs=(fr...  58.3 us
    pallas_call x1, Pallas kernels, shards(): pl.pallas_call(emit, out_shape=shapes, in_specs=[free] * 5, out_specs=(fr...  1.88 us

profile of v7, /device:TPU:8, one launch (start us, length us, event | category | flops | bytes accessed | tf_op | source)
XLA Modules:
  0.0 60.9 jit_solution(13796615553322064076)
XLA Ops:
  0.6 58.3 %shard_map.92 = (bf16[2,240,256]{2,1,0:T(8,128)(2,1)}, bf16[2,240,256]{2,1,0:T(8,128)(2,1)}, f32[3,240]{1,0:T(4,128)}, f32[2,32,128]{2,1,0:T(8,128)}, f32[1,64,256]{2,1,0:T(8,128)}) custom-call(bf16[2,240,256]{2,1,0:T(8,128)(2,1)} %x_in.1, bf16[2,128,128]{2,1,0:T(8,128)(2,1)} %f_in.1, bf16[1,256,256]{2,1,0:T(8,128)(2,1)} %s_in.1, f32[3,240]{1,0:T(4,128)} %k_in.1, ...), custom_call_target="tpu_custom_call" | custom-call | tf_op jit(solution)/shard_map/pallas_call | solution.py:435
  59.0 1.9 %shard_map.93 = (bf16[2,240,256]{2,1,0:T(8,128)(2,1)}, bf16[2,240,256]{2,1,0:T(8,128)(2,1)}, f32[3,240]{1,0:T(4,128)}, f32[2,32,128]{2,1,0:T(8,128)}, f32[1,64,256]{2,1,0:T(8,128)}) custom-call(bf16[2,240,256]{2,1,0:T(8,128)(2,1)} %get-tuple-element.10.refs_0_, bf16[2,240,256]{2,1,0:T(8,128)(2,1)} %get-tuple-element.11.refs_1_, ...), custom_call_target="tpu_custom_call" | custom-call | tf_op jit(solution)/shard_map/pallas_call | solution.py:469

commit v8 on v7

--- a/solution.py
+++ b/solution.py
@@ -271,6 +271,12 @@
     for b in range(BATCH):
         arrive(a1r.at[b], NX, A1 + b)
         over_x(nn(s11[...], flat(a1r, b)), a3s, a3r, b, A3)
+    for b in range(BATCH):
+        arrive(b2r.at[b], NL, B2 + b)
+        over_x(nn(tables[3], flat(b2r, b)), a2s, a2r, b, A2)
+        arrive(a3r.at[b], NX, A3 + b)
+        over_l(nn(tables[5], flat(a3r, b)), b3s, b3r, b, B3)
+
     grad = jnp.zeros((256, 256), F32)
     for b in range(BATCH):
         nat = nn(tables[6], flat(a1r, b)).astype(BF)
@@ -280,11 +286,6 @@
     half = lax.div(chan, 2)
     for h in range(2):
         remote(fgo.at[2 * h + 1 - core], fgp.at[h], (seq, 2 * half + 1 - core), FG).start()
-    for b in range(BATCH):
-        arrive(b2r.at[b], NL, B2 + b)
-        over_x(nn(tables[3], flat(b2r, b)), a2s, a2r, b, A2)
-        arrive(a3r.at[b], NX, A3 + b)
-        over_l(nn(tables[5], flat(a3r, b)), b3s, b3r, b, B3)
 
     prods = [jnp.zeros((ROWS, BLK), F32)] * 3
     for b in range(BATCH):
@@ -316,21 +317,23 @@
     pair = remote(fgs, fgr, (seq, 2 * (1 - half) + core), FH)
     pair.start()
 
+    parts = [jnp.zeros((BLK, BLK), F32)] * 2
     for b in range(BATCH):
         arrive(b3r.at[b], NL, B3 + b)
         mgr[b] = tn(flat(b3r, b), tables[1]).astype(BF)
+        for q in range(2):
+            lanes = slice(q * BLK, (q + 1) * BLK)
+            parts[q] = parts[q] + nn(xt[b, lanes, :], mgr[b, :, lanes])
+        if b == 0:
+            arrive(kxr, NX, KX)
+            kls[...] = sum((kxr[i] for i in range(1, NX)), kxr[0])
+            spread(kls, klr, ml, l_peer, NL, KL)
     for q in range(2):
-        lanes = slice(q * BLK, (q + 1) * BLK)
-        part = nn(xt[0, lanes, :], mgr[0, :, lanes]) + nn(xt[1, lanes, :], mgr[1, :, lanes])
-        part = part.reshape(CHAN, 32, BLK)
+        part = parts[q].reshape(CHAN, 32, BLK)
         for o in range(CHAN):
             bgo[o, q] = part[o]
             bgs[o, q] = part[o].astype(BF)
     scatter(bgs, bgr, chan, c_peer, CHAN, BG)
-
-    arrive(kxr, NX, KX)
-    kls[...] = sum((kxr[i] for i in range(1, NX)), kxr[0])
-    spread(kls, klr, ml, l_peer, NL, KL)
 
     far1 = hot((EXT, EXT), lambda r, c: r + 1 == c)
     far2 = hot((EXT, EXT), lambda r, c: r + 2 == c)

time: 61 us -> 61 us (level)
  the two profiles are of different devices: /device:TPU:8 before, /device:TPU:1 now
where the time goes in v8:
time: 61 us; the launch traced here: 60.6 us
  Pallas kernels  60 us (98%)
  between operations  0.64 us (1%)
    pallas_call x1, Pallas kernels, shards(): pl.pallas_call(body, out_shape=shapes, in_specs=[free] * 5, out_specs=(fr...  58.1 us
    pallas_call x1, Pallas kernels, shards(): pl.pallas_call(emit, out_shape=shapes, in_specs=[free] * 5, out_specs=(fr...  1.88 us

profile of v8, /device:TPU:1, one launch (start us, length us, event | category | flops | bytes accessed | tf_op | source)
XLA Modules:
  0.0 60.6 jit_solution(4666727800312336254)
XLA Ops:
  0.6 58.1 %shard_map.92 = (bf16[2,240,256]{2,1,0:T(8,128)(2,1)}, bf16[2,240,256]{2,1,0:T(8,128)(2,1)}, f32[3,240]{1,0:T(4,128)}, f32[2,32,128]{2,1,0:T(8,128)}, f32[1,64,256]{2,1,0:T(8,128)}) custom-call(bf16[2,240,256]{2,1,0:T(8,128)(2,1)} %x_in.1, bf16[2,128,128]{2,1,0:T(8,128)(2,1)} %f_in.1, bf16[1,256,256]{2,1,0:T(8,128)(2,1)} %s_in.1, f32[3,240]{1,0:T(4,128)} %k_in.1, ...), custom_call_target="tpu_custom_call" | custom-call | tf_op jit(solution)/shard_map/pallas_call | solution.py:438
  58.7 1.9 %shard_map.93 = (bf16[2,240,256]{2,1,0:T(8,128)(2,1)}, bf16[2,240,256]{2,1,0:T(8,128)(2,1)}, f32[3,240]{1,0:T(4,128)}, f32[2,32,128]{2,1,0:T(8,128)}, f32[1,64,256]{2,1,0:T(8,128)}) custom-call(bf16[2,240,256]{2,1,0:T(8,128)(2,1)} %get-tuple-element.10.refs_0_, bf16[2,240,256]{2,1,0:T(8,128)(2,1)} %get-tuple-element.11.refs_1_, ...), custom_call_target="tpu_custom_call" | custom-call | tf_op jit(solution)/shard_map/pallas_call | solution.py:472

commit v9 on v8

--- a/solution.py
+++ b/solution.py
@@ -236,8 +236,9 @@
     back = hot((256, 256), flip(order1))
     s11[...] = nt(nn(back, second).astype(BF), back).astype(BF)
 
-    arrive(a0r.at[0], NX, A0)
-    over_l(nn(tables[2], flat(a0r, 0)), b0s, b0r, 0, B0)
+    for b in range(BATCH):
+        arrive(a0r.at[b], NX, A0 + b)
+        over_l(nn(tables[2], flat(a0r, b)), b0s, b0r, b, B0)
 
     halo0.wait_recv()
     inside = (seq < SEQ - 1).astype(F32)
@@ -256,9 +257,6 @@
             remote(b1s.at[b, last], b1r.at[b, ml], (last * NX + mx, chan), B1 + b).start()
 
         keep(b1s.at[b], b1r.at[b], ml)
-
-    arrive(a0r.at[1], NX, A0 + 1)
-    over_l(nn(tables[2], flat(a0r, 1)), b0s, b0r, 1, B0)
 
     for b in range(BATCH):
         xt[b] = nt(eye, xs[b]).astype(BF)

time: 61 us -> 64.1 us (1.051)
  Pallas kernels: 60 us -> 63.3 us
    pallas_call x1, Pallas kernels: 58.1 us -> 61.4 us  [shards(): pl.pallas_call(body, out_shape=shapes, in_specs=[free] * 5, out_specs=(fr...]
where the time goes in v9:
time: 64.1 us; the launch traced here: 63.9 us
  Pallas kernels  63.3 us (99%)
    pallas_call x1, Pallas kernels, shards(): pl.pallas_call(body, out_shape=shapes, in_specs=[free] * 5, out_specs=(fr...  61.4 us
    pallas_call x1, Pallas kernels, shards(): pl.pallas_call(emit, out_shape=shapes, in_specs=[free] * 5, out_specs=(fr...  1.88 us

profile of v9, /device:TPU:1, one launch (start us, length us, event | category | flops | bytes accessed | tf_op | source)
XLA Modules:
  0.0 63.9 jit_solution(5510121046493265911)
XLA Ops:
  0.6 61.4 %shard_map.92 = (bf16[2,240,256]{2,1,0:T(8,128)(2,1)}, bf16[2,240,256]{2,1,0:T(8,128)(2,1)}, f32[3,240]{1,0:T(4,128)}, f32[2,32,128]{2,1,0:T(8,128)}, f32[1,64,256]{2,1,0:T(8,128)}) custom-call(bf16[2,240,256]{2,1,0:T(8,128)(2,1)} %x_in.1, bf16[2,128,128]{2,1,0:T(8,128)(2,1)} %f_in.1, bf16[1,256,256]{2,1,0:T(8,128)(2,1)} %s_in.1, f32[3,240]{1,0:T(4,128)} %k_in.1, ...), custom_call_target="tpu_custom_call" | custom-call | tf_op jit(solution)/shard_map/pallas_call | solution.py:436
  62.1 1.9 %shard_map.93 = (bf16[2,240,256]{2,1,0:T(8,128)(2,1)}, bf16[2,240,256]{2,1,0:T(8,128)(2,1)}, f32[3,240]{1,0:T(4,128)}, f32[2,32,128]{2,1,0:T(8,128)}, f32[1,64,256]{2,1,0:T(8,128)}) custom-call(bf16[2,240,256]{2,1,0:T(8,128)(2,1)} %get-tuple-element.10.refs_0_, bf16[2,240,256]{2,1,0:T(8,128)(2,1)} %get-tuple-element.11.refs_1_, ...), custom_call_target="tpu_custom_call" | custom-call | tf_op jit(solution)/shard_map/pallas_call | solution.py:470
